TPU v7x, 32 devices: a whole 2x2x4 slice. The times are simulated.
32 devices in a mesh: dp: 8 (over z, x), seq: 4 (over y, core).
Axes of the slice: x: 2, y: 2, z: 4, core: 2. Of those that a mesh axis runs over, the one named last changes fastest.
Arguments:
- media: bfloat16 [192, 128, 1536], P(('dp', 'seq')), may hold values from -6 to 6
- latents: bfloat16 [32, 64, 1536], P(('dp', 'seq')), may hold values from -6 to 6
- out_grad: bfloat16 [32, 64, 1536], P(('dp', 'seq')), may hold values from -6 to 6
- frame_counts: int32 [8, 4], P('dp'), may hold values from 1 to 8, 12 in all within a row
- block_position: int32 [8, 24], P('dp'), may hold values from 0 to 23, as said below
- w_query: bfloat16 [1536, 1536], P(('dp', 'seq')), may hold values from -0.3125 to 0.3125
- w_key: bfloat16 [1536, 1536], P(('dp', 'seq')), may hold values from -0.15625 to 0.15625
- w_value: bfloat16 [1536, 1536], P(('dp', 'seq')), may hold values from -0.15625 to 0.15625
- w_out: bfloat16 [1536, 1536], P(('dp', 'seq')), may hold values from -0.625 to 0.625
- w_up: bfloat16 [1536, 6144], P(('dp', 'seq')), may hold values from -0.15625 to 0.15625
- w_down: bfloat16 [6144, 1536], P(('dp', 'seq')), may hold values from -0.078125 to 0.078125
- gain_lat: bfloat16 [1536], P(('dp', 'seq')), may hold values from 0.5 to 1.5
- shift_lat: bfloat16 [1536], P(('dp', 'seq')), may hold values from -3 to 3
- gain_media: bfloat16 [1536], P(('dp', 'seq')), may hold values from 0.5 to 1.5
- shift_media: bfloat16 [1536], P(('dp', 'seq')), may hold values from -3 to 3
- gain_ffn: bfloat16 [1536], P(('dp', 'seq')), may hold values from 0.5 to 1.5
- shift_ffn: bfloat16 [1536], P(('dp', 'seq')), may hold values from -3 to 3
Outputs:
- latents_out: bfloat16 [32, 64, 1536], P(('dp', 'seq'))
- latents_grad: float32 [32, 64, 1536], P(('dp', 'seq'))
- media_grad: float32 [192, 128, 1536], P(('dp', 'seq'))
- grad_w_query: float32 [1536, 1536], P(('dp', 'seq'))
- grad_w_key: float32 [1536, 1536], P(('dp', 'seq'))
- grad_w_value: float32 [1536, 1536], P(('dp', 'seq'))
- grad_w_out: float32 [1536, 1536], P(('dp', 'seq'))
- grad_w_up: float32 [1536, 6144], P(('dp', 'seq'))
- grad_w_down: float32 [6144, 1536], P(('dp', 'seq'))
- grad_gain_lat: float32 [1536], P(('dp', 'seq'))
- grad_shift_lat: float32 [1536], P(('dp', 'seq'))
- grad_gain_media: float32 [1536], P(('dp', 'seq'))
- grad_shift_media: float32 [1536], P(('dp', 'seq'))
- grad_gain_ffn: float32 [1536], P(('dp', 'seq'))
- grad_shift_ffn: float32 [1536], P(('dp', 'seq'))
Inputs may be any that keep to these rules, and one draw needn't show every extreme that they name: `frame_counts`: row g gives the frames of the 4 items of group g in order; an item holds 2 blocks a frame; each row sums to 12 and its largest entry is 8. `block_position`: each row is a permutation of 0 to 23; the 6 blocks stored at seq index r all have positions with one common remainder modulo 4.
All inputs are finite; a program needn't handle non-finite values.
Results may differ from a plain program's by a relative error of at most 0.02.
Values may be sent and summed in bfloat16 or wider, within the bound.
A program may use at most 200 MiB of HBM per device.

v0:
```python
from functools import partial

import jax
import jax.numpy as jnp
from jax import lax
from jax.sharding import PartitionSpec as P

HEADS = 16
HEAD_DIM = 96
FRAME_BLOCKS = 2


EPS = 1e-05
NEG = -1e30
HIGH = lax.Precision.HIGHEST


def norm_forward(rows, gain, shift):
    mean = jnp.mean(rows, axis=-1, keepdims=True)
    centred = rows - mean
    variance = jnp.mean(centred * centred, axis=-1, keepdims=True)
    inverse = lax.rsqrt(variance + EPS)
    scaled = centred * inverse
    return (scaled * gain + shift, scaled, inverse)


def norm_backward(incoming, scaled, inverse, gain):
    inner = incoming * gain
    first = jnp.mean(inner, axis=-1, keepdims=True)
    second = jnp.mean(inner * scaled, axis=-1, keepdims=True)
    return (
        inverse * (inner - first - scaled * second),
        jnp.sum(incoming * scaled, axis=0),
        jnp.sum(incoming, axis=0),
    )


def matmul(left, right):
    return jnp.dot(left, right, preferred_element_type=jnp.float32)


def matmul_left_t(left, right):
    return lax.dot_general(
        left, right, (((0,), (0,)), ((), ())), preferred_element_type=jnp.float32
    )


def matmul_right_t(left, right):
    return lax.dot_general(
        left, right, (((1,), (1,)), ((), ())), preferred_element_type=jnp.float32
    )


def swap_rows(stat):
    return jnp.swapaxes(stat, 1, 2)[..., None]


def fold_sources(tops, totals, accums):
    best = jnp.max(tops, axis=0)
    factor = jnp.exp(tops - best[None])
    total = jnp.sum(factor * totals, axis=0)
    width = accums.shape[-1]
    spread = jnp.repeat(jnp.swapaxes(factor, 2, 3), width // factor.shape[2], axis=3)
    return (best, total, jnp.sum(accums * spread, axis=0))


def local(
    media,
    latents,
    out_grad,
    frame_counts,
    block_position,
    w_query,
    w_key,
    w_value,
    w_out,
    w_up,
    w_down,
    gain_lat,
    shift_lat,
    gain_media,
    shift_media,
    gain_ffn,
    shift_ffn,
):
    gathered = (
        lax.all_gather(w_query, ("dp", "seq"), axis=0, tiled=True),
        lax.all_gather(w_key, ("dp", "seq"), axis=0, tiled=True),
        lax.all_gather(w_value, ("dp", "seq"), axis=0, tiled=True),
        lax.all_gather(w_out, ("dp", "seq"), axis=0, tiled=True),
        lax.all_gather(w_up, ("dp", "seq"), axis=0, tiled=True),
        lax.all_gather(w_down, ("dp", "seq"), axis=0, tiled=True),
        lax.all_gather(gain_lat, ("dp", "seq"), axis=0, tiled=True),
        lax.all_gather(shift_lat, ("dp", "seq"), axis=0, tiled=True),
        lax.all_gather(gain_media, ("dp", "seq"), axis=0, tiled=True),
        lax.all_gather(shift_media, ("dp", "seq"), axis=0, tiled=True),
        lax.all_gather(gain_ffn, ("dp", "seq"), axis=0, tiled=True),
        lax.all_gather(shift_ffn, ("dp", "seq"), axis=0, tiled=True),
    )
    full_query, full_key, full_value, full_out, full_up, full_down = gathered[:6]
    lat_gain, lat_shift, med_gain, med_shift, ffn_gain, ffn_shift = [
        piece.astype(jnp.float32) for piece in gathered[6:]
    ]
    seq_rank = lax.axis_index("seq")
    seq_count = lax.axis_size("seq")
    blocks, block_rows, width = media.shape
    local_items, lat_rows, _ = latents.shape
    group_items = frame_counts.shape[1]
    heads = HEADS
    head_size = HEAD_DIM
    score_scale = head_size ** (-0.5)
    ends = FRAME_BLOCKS * jnp.cumsum(frame_counts[0])
    position = lax.dynamic_slice_in_dim(block_position[0], seq_rank * blocks, blocks)
    owner_item = jnp.sum((ends[None, :] <= position[:, None]).astype(jnp.int32), axis=1)
    member = (owner_item[:, None] == jnp.arange(group_items, dtype=jnp.int32)[None, :]).astype(
        jnp.float32
    )
    lat_input = latents.astype(jnp.float32).reshape(-1, width)
    normed_lat, scaled_lat, inverse_lat = norm_forward(lat_input, lat_gain, lat_shift)
    normed_lat = normed_lat.astype(jnp.bfloat16)
    query = matmul(normed_lat, full_query).astype(jnp.bfloat16)
    key_lat = (
        matmul(normed_lat, full_key)
        .astype(jnp.bfloat16)
        .reshape(local_items, lat_rows, heads, head_size)
    )
    value_lat = (
        matmul(normed_lat, full_value)
        .astype(jnp.bfloat16)
        .reshape(local_items, lat_rows, heads, head_size)
    )
    query_all = lax.all_gather(
        query.reshape(local_items, lat_rows, width), "seq", axis=0, tiled=True
    )
    med_input = media.astype(jnp.float32).reshape(-1, width)
    normed_med, scaled_med, inverse_med = norm_forward(med_input, med_gain, med_shift)
    normed_med = normed_med.astype(jnp.bfloat16)

    def media_keys(weight_key, weight_value):
        keys_out = (
            matmul(normed_med, weight_key)
            .astype(jnp.bfloat16)
            .reshape(blocks, block_rows, heads, head_size)
        )
        values_out = (
            matmul(normed_med, weight_value)
            .astype(jnp.bfloat16)
            .reshape(blocks, block_rows, heads, head_size)
        )
        return (keys_out, values_out)

    key_med, value_med = media_keys(full_key, full_value)
    query_blk = query_all[owner_item].reshape(blocks, lat_rows, heads, head_size)
    scores_med = (
        jnp.einsum("bqhd,bkhd->bhqk", query_blk, key_med, preferred_element_type=jnp.float32)
        * score_scale
    )
    block_top = jnp.max(scores_med, axis=-1)
    expo_med = jnp.exp(scores_med - block_top[..., None])
    expo_med_low = expo_med.astype(jnp.bfloat16)
    local_top = jnp.max(jnp.where(member.T[:, :, None, None] > 0, block_top[None], NEG), axis=1)
    to_local = jnp.exp(block_top - local_top[owner_item])
    local_total = jnp.einsum(
        "bi,bhq->ihq", member, to_local * jnp.sum(expo_med, axis=-1), precision=HIGH
    )
    accum_blk = jnp.einsum(
        "bhqk,bkhd->bqhd", expo_med_low, value_med, preferred_element_type=jnp.float32
    ) * swap_rows(to_local)
    local_accum = jnp.einsum("bi,bqhd->iqhd", member, accum_blk, precision=HIGH).reshape(
        group_items, lat_rows, width
    )
    part_top, part_total, part_accum = (
        lax.all_to_all(local_top, "seq", split_axis=0, concat_axis=0, tiled=True),
        lax.all_to_all(local_total, "seq", split_axis=0, concat_axis=0, tiled=True),
        lax.all_to_all(local_accum, "seq", split_axis=0, concat_axis=0, tiled=True),
    )
    top_own, total_own, accum_flat = fold_sources(
        part_top.reshape(seq_count, local_items, heads, lat_rows),
        part_total.reshape(seq_count, local_items, heads, lat_rows),
        part_accum.reshape(seq_count, local_items, lat_rows, width),
    )
    med_top = lax.all_gather(top_own, "seq", axis=0, tiled=True)
    accum_own = accum_flat.reshape(local_items, lat_rows, heads, head_size)
    query_lat = query.reshape(local_items, lat_rows, heads, head_size)
    scores_lat = (
        jnp.einsum("iqhd,ikhd->ihqk", query_lat, key_lat, preferred_element_type=jnp.float32)
        * score_scale
    )
    lat_top = jnp.max(scores_lat, axis=-1)
    expo_lat = jnp.exp(scores_lat - lat_top[..., None])
    expo_lat_low = expo_lat.astype(jnp.bfloat16)
    item_top = jnp.maximum(top_own, lat_top)
    media_weight = jnp.exp(top_own - item_top)
    lat_weight = jnp.exp(lat_top - item_top)
    item_total = total_own * media_weight + lat_weight * jnp.sum(expo_lat, axis=-1)
    inverse_total = 1.0 / item_total
    accum_lat = jnp.einsum(
        "ihqk,ikhd->iqhd", expo_lat_low, value_lat, preferred_element_type=jnp.float32
    ) * swap_rows(lat_weight)
    attended = (accum_own * swap_rows(media_weight) + accum_lat) * swap_rows(inverse_total)
    attended_low = attended.reshape(-1, width).astype(jnp.bfloat16)
    hidden = lat_input + matmul(attended_low, full_out)
    normed_ffn, scaled_ffn, inverse_ffn = norm_forward(hidden, ffn_gain, ffn_shift)
    normed_ffn = normed_ffn.astype(jnp.bfloat16)
    pre_act = matmul(normed_ffn, full_up)
    activated, gelu_back = jax.vjp(partial(jax.nn.gelu, approximate=False), pre_act)
    activated = activated.astype(jnp.bfloat16)
    result = hidden + matmul(activated, full_down)
    latents_out = result.astype(jnp.bfloat16).reshape(latents.shape)
    again = (
        lax.all_gather(w_query, ("dp", "seq"), axis=0, tiled=True),
        lax.all_gather(w_key, ("dp", "seq"), axis=0, tiled=True),
        lax.all_gather(w_value, ("dp", "seq"), axis=0, tiled=True),
        lax.all_gather(w_out, ("dp", "seq"), axis=0, tiled=True),
        lax.all_gather(w_up, ("dp", "seq"), axis=0, tiled=True),
        lax.all_gather(w_down, ("dp", "seq"), axis=0, tiled=True),
        lax.all_gather(gain_lat, ("dp", "seq"), axis=0, tiled=True),
        lax.all_gather(shift_lat, ("dp", "seq"), axis=0, tiled=True),
        lax.all_gather(gain_media, ("dp", "seq"), axis=0, tiled=True),
        lax.all_gather(shift_media, ("dp", "seq"), axis=0, tiled=True),
        lax.all_gather(gain_ffn, ("dp", "seq"), axis=0, tiled=True),
        lax.all_gather(shift_ffn, ("dp", "seq"), axis=0, tiled=True),
    )
    back_query, back_key, back_value, back_out, back_up, back_down = again[:6]
    grad_rows = out_grad.reshape(-1, width)
    cotangent = grad_rows.astype(jnp.float32)
    grad_down = matmul_left_t(activated, grad_rows)
    grad_act = matmul_right_t(grad_rows, back_down)
    grad_pre = gelu_back(grad_act)[0].astype(jnp.bfloat16)
    grad_up = matmul_left_t(normed_ffn, grad_pre)
    grad_normed_ffn = matmul_right_t(grad_pre, back_up)
    grad_hidden_norm, grad_gain_ffn, grad_shift_ffn = norm_backward(
        grad_normed_ffn, scaled_ffn, inverse_ffn, ffn_gain
    )
    grad_hidden = cotangent + grad_hidden_norm
    grad_hidden_low = grad_hidden.astype(jnp.bfloat16)
    grad_out = matmul_left_t(attended_low, grad_hidden_low)
    grad_att = matmul_right_t(grad_hidden_low, back_out).astype(jnp.bfloat16)
    grad_att_heads = grad_att.reshape(local_items, lat_rows, heads, head_size)
    delta = jnp.einsum(
        "iqhd,iqhd->ihq", grad_att_heads.astype(jnp.float32), attended, precision=HIGH
    )
    media_factor = media_weight * inverse_total
    grad_att_all = lax.all_gather(
        grad_att.reshape(local_items, lat_rows, width), "seq", axis=0, tiled=True
    )
    factor_all, delta_all = (
        lax.all_gather(media_factor, "seq", axis=0, tiled=True),
        lax.all_gather(delta, "seq", axis=0, tiled=True),
    )
    key_med, value_med = media_keys(back_key, back_value)
    grad_blk = grad_att_all[owner_item].reshape(blocks, lat_rows, heads, head_size)
    factor_blk = jnp.exp(block_top - med_top[owner_item]) * factor_all[owner_item]
    delta_blk = delta_all[owner_item]
    grad_prob_med = jnp.einsum(
        "bqhd,bkhd->bhqk", grad_blk, value_med, preferred_element_type=jnp.float32
    )
    grad_score_med = (
        expo_med * factor_blk[..., None] * (grad_prob_med - delta_blk[..., None])
    ).astype(jnp.bfloat16)
    grad_query_blk = (
        jnp.einsum("bhqk,bkhd->bqhd", grad_score_med, key_med, preferred_element_type=jnp.float32)
        * score_scale
    )
    grad_query_part = jnp.einsum("bi,bqhd->iqhd", member, grad_query_blk, precision=HIGH).reshape(
        group_items, lat_rows, width
    )
    grad_key_med = (
        (
            jnp.einsum(
                "bhqk,bqhd->bkhd", grad_score_med, query_blk, preferred_element_type=jnp.float32
            )
            * score_scale
        )
        .astype(jnp.bfloat16)
        .reshape(-1, width)
    )
    grad_value_med = (
        jnp.einsum(
            "bhqk,bqhd->bkhd",
            expo_med_low.astype(jnp.float32) * factor_blk[..., None],
            grad_blk.astype(jnp.float32),
            precision=HIGH,
        )
        .astype(jnp.bfloat16)
        .reshape(-1, width)
    )
    grad_query_own = lax.psum_scatter(
        grad_query_part.astype(jnp.bfloat16), "seq", scatter_dimension=0, tiled=True
    ).astype(jnp.float32)
    grad_normed_med = matmul_right_t(grad_key_med, back_key) + matmul_right_t(
        grad_value_med, back_value
    )
    grad_key = matmul_left_t(normed_med, grad_key_med)
    grad_value = matmul_left_t(normed_med, grad_value_med)
    media_grad, grad_gain_media, grad_shift_media = norm_backward(
        grad_normed_med, scaled_med, inverse_med, med_gain
    )
    lat_factor = lat_weight * inverse_total
    grad_prob_lat = jnp.einsum(
        "iqhd,ikhd->ihqk", grad_att_heads, value_lat, preferred_element_type=jnp.float32
    )
    grad_score_lat = (expo_lat * lat_factor[..., None] * (grad_prob_lat - delta[..., None])).astype(
        jnp.bfloat16
    )
    grad_query_lat = (
        jnp.einsum("ihqk,ikhd->iqhd", grad_score_lat, key_lat, preferred_element_type=jnp.float32)
        * score_scale
    )
    grad_key_lat = (
        (
            jnp.einsum(
                "ihqk,iqhd->ikhd", grad_score_lat, query_lat, preferred_element_type=jnp.float32
            )
            * score_scale
        )
        .astype(jnp.bfloat16)
        .reshape(-1, width)
    )
    grad_value_lat = (
        jnp.einsum(
            "ihqk,iqhd->ikhd",
            expo_lat_low.astype(jnp.float32) * lat_factor[..., None],
            grad_att_heads.astype(jnp.float32),
            precision=HIGH,
        )
        .astype(jnp.bfloat16)
        .reshape(-1, width)
    )
    grad_query = (
        (grad_query_own + grad_query_lat.reshape(local_items, lat_rows, width))
        .astype(jnp.bfloat16)
        .reshape(-1, width)
    )
    grad_normed_lat = (
        matmul_right_t(grad_query, back_query)
        + matmul_right_t(grad_key_lat, back_key)
        + matmul_right_t(grad_value_lat, back_value)
    )
    grad_query_weight = matmul_left_t(normed_lat, grad_query)
    grad_key = grad_key + matmul_left_t(normed_lat, grad_key_lat)
    grad_value = grad_value + matmul_left_t(normed_lat, grad_value_lat)
    grad_lat_norm, grad_gain_lat, grad_shift_lat = norm_backward(
        grad_normed_lat, scaled_lat, inverse_lat, lat_gain
    )
    latents_grad = (grad_hidden + grad_lat_norm).reshape(latents.shape)
    sharded = (
        lax.psum_scatter(grad_query_weight, ("dp", "seq"), scatter_dimension=0, tiled=True),
        lax.psum_scatter(grad_key, ("dp", "seq"), scatter_dimension=0, tiled=True),
        lax.psum_scatter(grad_value, ("dp", "seq"), scatter_dimension=0, tiled=True),
        lax.psum_scatter(grad_out, ("dp", "seq"), scatter_dimension=0, tiled=True),
        lax.psum_scatter(grad_up, ("dp", "seq"), scatter_dimension=0, tiled=True),
        lax.psum_scatter(grad_down, ("dp", "seq"), scatter_dimension=0, tiled=True),
        lax.psum_scatter(grad_gain_lat, ("dp", "seq"), scatter_dimension=0, tiled=True),
        lax.psum_scatter(grad_shift_lat, ("dp", "seq"), scatter_dimension=0, tiled=True),
        lax.psum_scatter(grad_gain_media, ("dp", "seq"), scatter_dimension=0, tiled=True),
        lax.psum_scatter(grad_shift_media, ("dp", "seq"), scatter_dimension=0, tiled=True),
        lax.psum_scatter(grad_gain_ffn, ("dp", "seq"), scatter_dimension=0, tiled=True),
        lax.psum_scatter(grad_shift_ffn, ("dp", "seq"), scatter_dimension=0, tiled=True),
    )
    return (latents_out, latents_grad, media_grad.reshape(media.shape)) + tuple(sharded)


def solution(mesh):
    return jax.shard_map(
        local,
        mesh=mesh,
        in_specs=(
            P(("dp", "seq"), None, None),
            P(("dp", "seq"), None, None),
            P(("dp", "seq"), None, None),
            P("dp", None),
            P("dp", None),
            P(("dp", "seq"), None),
            P(("dp", "seq"), None),
            P(("dp", "seq"), None),
            P(("dp", "seq"), None),
            P(("dp", "seq"), None),
            P(("dp", "seq"), None),
            P(("dp", "seq")),
            P(("dp", "seq")),
            P(("dp", "seq")),
            P(("dp", "seq")),
            P(("dp", "seq")),
            P(("dp", "seq")),
        ),
        out_specs=(
            P(("dp", "seq"), None, None),
            P(("dp", "seq"), None, None),
            P(("dp", "seq"), None, None),
            P(("dp", "seq"), None),
            P(("dp", "seq"), None),
            P(("dp", "seq"), None),
            P(("dp", "seq"), None),
            P(("dp", "seq"), None),
            P(("dp", "seq"), None),
            P(("dp", "seq")),
            P(("dp", "seq")),
            P(("dp", "seq")),
            P(("dp", "seq")),
            P(("dp", "seq")),
            P(("dp", "seq")),
        ),
        check_vma=False,
    )
```

profile of v0, /device:TPU:0, one launch (start us, length us, event | category | flops | bytes accessed | tf_op | source)
XLA Modules:
  0.0 1909.3 jit_solution(7601242279144891453)
XLA Ops:
  12.8 42.4 %all-reduce.13 = (bf16[1536]{0:T(1024)(128)(2,1)S(1)}, bf16[1536]{0:T(1024)(128)(2,1)S(1)}, bf16[1536]{0:T(1024)(128)(2,1)S(1)}, bf16[1536]{0:T(1024)(128)(2,1)S...) all-reduce(bf16[1536]{0:T(1024)(128)(2,1)S(1)} %dynamic-update-slic, ...), channel_id=1, replica_groups=mesh['dp'=8,'seq'=4] {'dp','seq'}, use_global_device_ids=true, to_apply=%add.1 | all-reduce | flops 9216 | bytes 36864
  64.5 12.9 all-gather.15.cloned.1.call-done
  77.4 8.3 convolution_convert_fusion
  85.7 4.9 reshape.598
  90.6 3.2 copy.114
  93.8 49.0 %all-gather.13.cloned.1.call-done = bf16[1536,1536]{1,0:T(8,128)(2,1)} async-done(((bf16[48,1536]{1,0:T(8,128)(2,1)}), bf16[1536,1536]{1,0:T(8,128)(2,1)}) %all-gather.13.cloned.1.call-update) | async-done | bytes 4718608 | tf_op jit(solution)/shard_map/all_gather | solution.py:87
  142.8 3.3 convolution_convert_fusion.5
  146.1 8.8 all-gather
  157.8 3.2 multiply_reduce_fusion.4
  163.1 3.3 all-to-all-start.1
  166.3 41.8 %all-gather.11.cloned.1.call-done = bf16[1536,1536]{1,0:T(8,128)(2,1)} async-done(((bf16[48,1536]{1,0:T(8,128)(2,1)}), bf16[1536,1536]{1,0:T(8,128)(2,1)}) %all-gather.11.cloned.1.call-update) | async-done | bytes 4718608 | tf_op jit(solution)/shard_map/all_gather | solution.py:89
  208.1 8.3 convolution_convert_fusion.1
  216.4 6.1 reshape.595
  222.4 4.8 copy.115
  229.1 4.2 convolution_convert_fusion.4
  233.3 2.6 bitcast_multiply_fusion
  235.9 5.7 fusion.3
  242.5 3.7 all-to-all-start.2
  246.2 4.0 convolution_convert_fusion.3
  255.8 3.1 copy.117
  258.9 3.1 reshape.599
  262.0 4.4 all-to-all-start
  275.3 3.1 broadcast_in_dim.21
  279.1 8.3 all_gather.71
  288.6 5.2 all-gather.1
  295.8 2.9 multiply_reduce_fusion.5
  300.7 2.7 fusion.133
  306.2 3.5 fusion.134
  310.6 89.0 %all-gather.19.cloned.1.call-done = bf16[1536,6144]{1,0:T(8,128)(2,1)} async-done(((bf16[48,6144]{1,0:T(8,128)(2,1)}), bf16[1536,6144]{1,0:T(8,128)(2,1)}) %all-gather.19.cloned.1.call-update) | async-done | bytes 18874384 | tf_op jit(solution)/shard_map/all_gather | solution.py:91
  399.6 11.1 fusion.125
  410.8 114.5 %all-gather.21.cloned.1.call-done = bf16[6144,1536]{1,0:T(8,128)(2,1)} async-done(((bf16[192,1536]{1,0:T(8,128)(2,1)}), bf16[6144,1536]{1,0:T(8,128)(2,1)}) %all-gather.21.cloned.1.call-update) | async-done | bytes 18874384 | tf_op jit(solution)/shard_map/all_gather | solution.py:92
  525.3 12.8 add_convert_fusion.2
  538.1 13.8 multiply_reduce_fusion.6
  554.0 4.5 convolution_convert_fusion.2
  560.4 10.7 all-gather.2
  572.4 5.2 all-gather.3
  578.8 2.8 gather_fusion.4
  581.6 4.0 reshape.607
  585.5 4.3 multiply_convert_fusion.1
  595.3 4.5 fusion.22
  600.9 2.9 convert_element_type.194
  607.9 5.1 copy.143
  613.0 6.4 reshape.615
  619.4 6.3 fusion.136
  625.7 5.1 convolution_add_fusion.1
  635.3 6.6 convert_bitcast_fusion
  641.9 3.7 copy.145
  645.6 4.5 reshape.616
  650.1 6.5 fusion.137
  656.6 5.1 convolution_add_fusion
  662.9 5.0 fusion.83
  669.8 6.1 fusion.120
  677.2 15.7 fusion.124
  694.3 16.7 fusion.77
  711.0 6.8 fusion.135
  717.8 7.3 multiply_reduce_fusion
  725.2 3.2 subtract_multiply_fusion
  728.4 11.9 fusion.10
  745.2 39.4 %all-reduce.12 = (f32[1536]{0:T(1024)S(1)}, f32[1536]{0:T(1024)S(1)}, f32[1536]{0:T(1024)S(1)}, f32[1536]{0:T(1024)S(1)}, f32[1536]{0:T(1024)S(1)}, /*index=5*/f32[1536]{0:T(1024)S(1)}) all-reduce(f32[1536]{0:T(1024)S(1)} %get-tuple-element.21, f32[1536]{0:T(1024)S(1)} %get-tuple-element.26, ...), channel_id=13, replica_groups=mesh['dp'=8,'seq'=4] {'dp','seq'}, use_global_device_ids=true, to_apply=%region_30.31.clone | all-reduce | flops 9216 | bytes 73728
  789.1 120.4 %reduce-scatter.14.cloned.1.call-done = f32[48,1536]{1,0:T(8,128)} async-done(((f32[1536,1536]{1,0:T(8,128)}), f32[48,1536]{1,0:T(8,128)}) %reduce-scatter.14.cloned.1.call-update) | async-done | bytes 294928 | tf_op jit(solution)/shard_map/reduce_scatter | solution.py:350
  909.5 141.8 %reduce-scatter.16.cloned.1.call-done = f32[48,1536]{1,0:T(8,128)} async-done(((f32[1536,1536]{1,0:T(8,128)}), f32[48,1536]{1,0:T(8,128)}) %reduce-scatter.16.cloned.1.call-update) | async-done | bytes 294928 | tf_op jit(solution)/shard_map/reduce_scatter | solution.py:351
  1051.3 141.1 %reduce-scatter.10.cloned.1.call-done = f32[48,1536]{1,0:T(8,128)} async-done(((f32[1536,1536]{1,0:T(8,128)}), f32[48,1536]{1,0:T(8,128)}) %reduce-scatter.10.cloned.1.call-update) | async-done | bytes 294928 | tf_op jit(solution)/shard_map/reduce_scatter | solution.py:348
  1192.4 355.5 %reduce-scatter.18.cloned.1.call-done = f32[48,6144]{1,0:T(8,128)} async-done(((f32[1536,6144]{1,0:T(8,128)}), f32[48,6144]{1,0:T(8,128)}) %reduce-scatter.18.cloned.1.call-update) | async-done | bytes 1179664 | tf_op jit(solution)/shard_map/reduce_scatter | solution.py:352
  1547.9 354.5 %reduce-scatter.20.cloned.1.call-done = f32[192,1536]{1,0:T(8,128)} async-done(((f32[6144,1536]{1,0:T(8,128)}), f32[192,1536]{1,0:T(8,128)}) %reduce-scatter.20.cloned.1.call-update) | async-done | bytes 1179664 | tf_op jit(solution)/shard_map/reduce_scatter | solution.py:353
  (268 shorter events, 82.5 us)
Async XLA Ops:
  7.2 48.9 %copy-start = (s32[1,24]{1,0:T(1,128)S(1)}, s32[1,24]{1,0:T(1,128)}, u32[]{:S(2)}) copy-start(s32[1,24]{1,0:T(1,128)} %param.21) | copy-start | bytes 292
  7.2 4.1 copy-start.52
  7.2 4.3 copy-start.53
  7.2 4.6 copy-start.54
  7.2 4.8 copy-start.55
  7.2 5.1 copy-start.56
  7.2 5.3 copy-start.57
  7.3 48.0 %copy-start.58 = (s32[1,4]{1,0:T(1,128)S(1)}, s32[1,4]{1,0:T(1,128)}, u32[]{:S(2)}) copy-start(s32[1,4]{1,0:T(1,128)} %param.20) | copy-start | bytes 52
  7.3 49.0 %copy-start.4 = (bf16[1,64,1536]{2,1,0:T(8,128)(2,1)S(1)}, bf16[1,64,1536]{2,1,0:T(8,128)(2,1)}, u32[]{:S(2)}) copy-start(bf16[1,64,1536]{2,1,0:T(8,128)(2,1)} %param.18) | copy-start | bytes 589828
  7.3 70.1 %all-gather.15.cloned.1.call-start = ((), (), s32[]{:S(2)}) async-start(), calls=%async_computation.12 | async-start | bytes 4866048 | tf_op jit(solution)/shard_map/all_gather | solution.py:88
  8.0 134.7 %all-gather.13.cloned.1.call-start = ((), (), s32[]{:S(2)}) async-start(), calls=%async_computation.11 | async-start | bytes 4866048 | tf_op jit(solution)/shard_map/all_gather | solution.py:87
  8.8 199.3 %all-gather.11.cloned.1.call-start = ((), (), s32[]{:S(2)}) async-start(), calls=%async_computation.10 | async-start | bytes 4866048 | tf_op jit(solution)/shard_map/all_gather | solution.py:89
  9.5 296.7 %all-gather.17.cloned.1.call-start = ((), (), s32[]{:S(2)}) async-start(), calls=%async_computation.13 | async-start | bytes 4866048 | tf_op jit(solution)/shard_map/all_gather | solution.py:90
  10.1 389.5 %all-gather.19.cloned.1.call-start = ((), (), s32[]{:S(2)}) async-start(), calls=%async_computation.14 | async-start | bytes 19464192 | tf_op jit(solution)/shard_map/all_gather | solution.py:91
  10.7 514.6 %all-gather.21.cloned.1.call-start = ((), (), s32[]{:S(2)}) async-start(), calls=%async_computation.15 | async-start | bytes 19464192 | tf_op jit(solution)/shard_map/all_gather | solution.py:92
  11.2 47.8 %copy-start.2 = (bf16[6,128,1536]{2,1,0:T(8,128)(2,1)S(1)}, bf16[6,128,1536]{2,1,0:T(8,128)(2,1)}, u32[]{:S(2)}) copy-start(bf16[6,128,1536]{2,1,0:T(8,128)(2,1)} %param.17) | copy-start | bytes 7077892
  55.2 7.0 copy-start.35
  56.2 185.4 %copy-start.50 = (s32[6]{0:T(128)}, s32[6]{0:T(128)S(1)}, u32[]{:S(2)}) copy-start(s32[6]{0:T(128)S(1)} %convert_reduce_fusion.2) | copy-start | bytes 76
  56.2 105.6 %copy-start.48 = (s32[1024]{0:T(1024)}, s32[1024]{0:T(1024)S(1)}, u32[]{:S(2)}) copy-start(s32[1024]{0:T(1024)S(1)} %pad_clamp_fusion) | copy-start | bytes 12292
  56.6 613.2 %copy-start.39 = (f32[64]{0:T(128)}, f32[64]{0:T(128)S(1)}, u32[]{:S(2)}) copy-start(f32[64]{0:T(128)S(1)} %add_rsqrt_fusion.2) | copy-start | bytes 772
  59.0 3.1 copy-start.41
  59.8 2.4 copy-start.43
  146.1 8.9 copy-start.24
  163.1 79.5 %all-to-all-start.1 = ((f32[4,1,1024]{2,1,0:T(1,128)}), f32[4,1,1024]{2,1,0:T(1,128)S(1)}, u32[]{:S(2)}, u32[]{:S(2)}) async-start(f32[4,1,1024]{2,1,0:T(1,128)} %reshape.687), calls=%async_computation.1 | async-start | bytes 32768 | tf_op jit(solution)/shard_map/all_to_all | solution.py:173
  229.1 4.2 copy-start.9
  242.5 19.4 %all-to-all-start.2 = ((f32[4,1,1024]{2,1,0:T(1,128)}), f32[4,1,1024]{2,1,0:T(1,128)S(1)}, u32[]{:S(2)}, u32[]{:S(2)}) async-start(f32[4,1,1024]{2,1,0:T(1,128)} %reshape.689), calls=%async_computation.2 | async-start | bytes 32768 | tf_op jit(solution)/shard_map/all_to_all | solution.py:174
  262.0 33.9 %all-to-all-start = ((f32[4,64,1536]{2,1,0:T(8,128)}), f32[4,64,1536]{2,1,0:T(8,128)}, u32[]{:S(2)}, u32[]{:S(2)}) async-start(f32[4,64,1536]{2,1,0:T(8,128)} %reshape.599), calls=%async_computation | async-start | bytes 3145728 | tf_op jit(solution)/shard_map/all_to_all | solution.py:175
  266.3 403.5 %reduce-scatter.8.cloned.1.call-start = ((), (), s32[]{:S(2)}) async-start(), calls=%async_computation.16 | async-start | bytes 983040 | tf_op jit(solution)/shard_map/reduce_scatter | solution.py:288
  267.7 4.8 copy-start.30
  275.3 3.1 copy-start.31
  275.3 3.1 copy-start.33
  275.3 3.2 copy-start.37
  275.3 3.2 copy-start.38
  275.3 12.1 copy-start.49
  295.8 4.9 copy-start.47
  306.2 93.4 %copy-start.29 = (f32[1536]{0:T(1024)S(1)}, f32[1536]{0:T(1024)}, u32[]{:S(2)}) copy-start(f32[1536]{0:T(1024)} %convert_element_type.184) | copy-start | bytes 18436
  560.4 11.7 copy-start.20
  585.5 4.4 copy-start.5
  589.9 1.9 copy-start.8
  591.8 2.5 copy-start.11
  591.8 2.5 copy-start.17
  591.8 2.5 copy-start.26
  591.8 3.5 copy-start.51
  603.8 185.3 %reduce-scatter.12.cloned.1.call-start = ((), (), s32[]{:S(2)}) async-start(), calls=%async_computation.18 | async-start | bytes 9732096 | tf_op jit(solution)/shard_map/reduce_scatter | solution.py:349
  619.4 6.3 copy-start.21
  630.9 278.6 %reduce-scatter.14.cloned.1.call-start = ((), (), s32[]{:S(2)}) async-start(), calls=%async_computation.19 | async-start | bytes 9732096 | tf_op jit(solution)/shard_map/reduce_scatter | solution.py:350
  650.1 6.5 copy-start.23
  661.8 389.5 %reduce-scatter.16.cloned.1.call-start = ((), (), s32[]{:S(2)}) async-start(), calls=%async_computation.20 | async-start | bytes 9732096 | tf_op jit(solution)/shard_map/reduce_scatter | solution.py:351
  667.9 524.5 %reduce-scatter.10.cloned.1.call-start = ((), (), s32[]{:S(2)}) async-start(), calls=%async_computation.17 | async-start | bytes 9732096 | tf_op jit(solution)/shard_map/reduce_scatter | solution.py:348
  675.9 871.9 %reduce-scatter.18.cloned.1.call-start = ((), (), s32[]{:S(2)}) async-start(), calls=%async_computation.21 | async-start | bytes 38928384 | tf_op jit(solution)/shard_map/reduce_scatter | solution.py:352
  692.9 1209.5 %reduce-scatter.20.cloned.1.call-start = ((), (), s32[]{:S(2)}) async-start(), calls=%async_computation.22 | async-start | bytes 38928384 | tf_op jit(solution)/shard_map/reduce_scatter | solution.py:353
  711.0 6.8 copy-start.3
  711.0 6.8 copy-start.19
  711.0 6.8 copy-start.36
  711.0 6.8 copy-start.42
  711.0 6.8 copy-start.44
  725.2 15.1 slice-start.2
  725.2 16.7 slice-start
  725.2 18.3 slice-start.4
  728.4 11.9 slice-start.3
  728.4 11.9 copy-start.27
  728.4 13.5 slice-start.1
  728.4 15.1 slice-start.5
  743.5 1158.8 %copy-start.1 = (s32[1,24]{1,0:T(1,128)S(1)}, s32[1,24]{1,0:T(1,128)}, u32[]{:S(2)}) copy-start(s32[1,24]{1,0:T(1,128)} %param.21) | copy-start | bytes 292
  (17 other events, 21.1 us)
Sparse Core Ops, SparseCore 0:
  11.0 66.3 all-gather.14
  80.3 62.3 all-gather.12
  145.7 62.3 all-gather.10
  210.9 62.4 all-gather.16
  276.1 123.4 all-gather.18
  402.4 122.8 all-gather.20
  604.0 21.3 reduce-scatter.7
  632.9 135.4 reduce-scatter.11
  774.8 134.6 reduce-scatter.13
  916.8 134.4 reduce-scatter.15
  1057.8 134.5 reduce-scatter.9
  1200.4 347.4 reduce-scatter.17
  1554.9 347.4 reduce-scatter.19
where the time goes:
time: 1920 us; the launch traced here: 1910 us
  waiting for transfers between devices  1420 us (74%)
  matrix products  211 us (11%)
  blocking collectives  120 us (6%)
  local copies, waits for them, and re-layouts  102 us (5%)
  other arithmetic  25.8 us (1%)
    reduce_scatter x1, waiting for transfers between devices, local(): lax.psum_scatter(grad_up, ('dp', 'seq'), scatter_dimension=0, tiled=True)  355 us
    reduce_scatter x1, waiting for transfers between devices, local(): lax.psum_scatter(grad_down, ('dp', 'seq'), scatter_dimension=0, tiled=True)  354 us
    reduce_scatter x1, waiting for transfers between devices, local(): lax.psum_scatter(grad_out, ('dp', 'seq'), scatter_dimension=0, tiled=True)  142 us
    reduce_scatter x1, waiting for transfers between devices, local(): lax.psum_scatter(grad_query_weight, ('dp', 'seq'), scatter_dimension=0, t...  141 us
    reduce_scatter x1, waiting for transfers between devices, local(): lax.psum_scatter(grad_value, ('dp', 'seq'), scatter_dimension=0, tiled=True)  120 us
    all_gather x1, waiting for transfers between devices, local(): lax.all_gather(w_down, ('dp', 'seq'), axis=0, tiled=True)  114 us
    all_gather x1, waiting for transfers between devices, local(): lax.all_gather(w_up, ('dp', 'seq'), axis=0, tiled=True)  89 us
    unnamed x2, blocking collectives  81.8 us
  transfers between devices with their start and end apart: 16, of which 10 were waited for; matrix products, arithmetic and copies ran while one was open for 14% of the time, Pallas kernels for 0%

commit v1 on v0

--- a/solution.py
+++ b/solution.py
@@ -1,18 +1,1157 @@
 from functools import partial
-
+from jax.sharding import PartitionSpec as P
+import functools
 import jax
 import jax.numpy as jnp
 from jax import lax
-from jax.sharding import PartitionSpec as P
+from jax.experimental import pallas as pl
+from jax.experimental.pallas import tpu as pltpu
+
+MESH = pl.DeviceIdType.MESH
+ANY = pl.BlockSpec(memory_space=pl.ANY)
+VMEM = pl.BlockSpec(memory_space=pltpu.VMEM)
+DMA = pltpu.SemaphoreType.DMA
+
+
+class Here:
+    def __init__(self, dp_count):
+        dp, seq = lax.axis_index("dp"), lax.axis_index("seq")
+        self.nz = dp_count // 2
+        self.z, self.x, self.y, self.c = dp // 2, dp % 2, seq // 2, seq % 2
+        self.dp, self.seq = dp, seq
+
+    def at(self, z=None, x=None, y=None, c=None):
+        z = self.z if z is None else z
+        x = self.x if x is None else x
+        y = self.y if y is None else y
+        c = self.c if c is None else c
+        return (z * 2 + x, y * 2 + c)
+
+
+def send(src, dst, ss, rs, to):
+    copy = pltpu.make_async_remote_copy(
+        src_ref=src, dst_ref=dst, send_sem=ss, recv_sem=rs, device_id=to, device_id_type=MESH
+    )
+    copy.start()
+
+
+def landed(dst, ss, rs, me):
+    pltpu.make_async_remote_copy(
+        src_ref=dst, dst_ref=dst, send_sem=ss, recv_sem=rs, device_id=me.at(c=1 - me.c), device_id_type=MESH
+    ).wait_recv()
+
+
+def sent(src, ss, rs, me):
+    pltpu.make_async_remote_copy(
+        src_ref=src, dst_ref=src, send_sem=ss, recv_sem=rs, device_id=me.at(c=1 - me.c), device_id_type=MESH
+    ).wait_send()
+
+
+def greet(devices):
+    barrier = pltpu.get_barrier_semaphore()
+    for device in devices:
+        pl.semaphore_signal(barrier, inc=1, device_id=device, device_id_type=MESH)
+    pl.semaphore_wait(barrier, len(devices))
+
+
+COL, FROMX, FROMY, DIAGA, DIAGB = range(5)
+TOUP, TODOWN, TOX, TOY, FWDY, FWDX, TOC = range(7)
+RECV_KINDS, SEND_KINDS = 10, 12
+
+
+class Gather:
+    def __init__(self, me, src, dst, ss, rs, axes, halves):
+        self.me, self.src, self.dst, self.ss, self.rs = me, src, dst, ss, rs
+        self.axes, self.halves = axes, halves
+        self.sends = []
+        self.depth = me.nz if "z" in axes else 1
+
+    def slot(self, z, x, y, c):
+        if self.axes == "zxyc":
+            return ((z * 2 + x) * 2 + y) * 2 + c
+        if self.axes == "zx":
+            return z * 2 + x
+        return y * 2 + c
+
+    def shard(self, z, x, y, c, half=None):
+        ref = self.dst.at[self.slot(z, x, y, c)]
+        if half is None or not self.halves:
+            return ref
+        width = self.halves
+        return ref.at[:, pl.ds(0, width)] if half == 0 else ref.at[:, pl.ds(width, width)]
+
+    def key(self, z):
+        return z if "z" in self.axes else 0
+
+    def start(self, src, dst, out_kind, in_kind, z, to):
+        k = self.key(z)
+        send(src, dst, self.ss.at[out_kind, k], self.rs.at[in_kind, k], to)
+
+    def hand_over(self, ref, kind, z):
+        if "c" in self.axes:
+            self.start(ref, ref, TOC + kind, 5 + kind, z, self.me.at(c=1 - self.me.c))
+
+    def spread(self, ref, z):
+        me = self.me
+        if "x" in self.axes:
+            self.start(ref, ref, TOX, FROMX, z, me.at(x=1 - me.x))
+        if "y" in self.axes:
+            self.start(ref, ref, TOY, FROMY, z, me.at(y=1 - me.y))
+        self.hand_over(ref, COL, z)
+
+    def own(self):
+        me = self.me
+        ref = self.shard(me.z, me.x, me.y, me.c)
+        if "z" in self.axes:
+            @pl.when(me.z + 1 < me.nz)
+            def _():
+                self.start(self.src, ref, TOUP, COL, me.z, me.at(z=me.z + 1))
+
+            @pl.when(me.z > 0)
+            def _():
+                self.start(self.src, ref, TODOWN, COL, me.z, me.at(z=me.z - 1))
+        if "x" in self.axes:
+            self.start(self.src, ref, TOX, FROMX, me.z, me.at(x=1 - me.x))
+        if "y" in self.axes:
+            self.start(self.src, ref, TOY, FROMY, me.z, me.at(y=1 - me.y))
+        if "c" in self.axes:
+            self.start(self.src, ref, TOC, 5, me.z, me.at(c=1 - me.c))
+
+    def around(self, event):
+        me = self.me
+        event(me.z)
+        for d in range(1, self.depth):
+            pl.when(me.z >= d)(functools.partial(event, me.z - d))
+            pl.when(me.z + d < me.nz)(functools.partial(event, me.z + d))
+
+    def column(self):
+        me = self.me
+        for d in range(1, self.depth):
+            for below in (True, False):
+                there = me.z - d if below else me.z + d
+                ahead = me.z + 1 if below else me.z - 1
+
+                @pl.when(there >= 0 if below else there < me.nz)
+                def _():
+                    ref = self.shard(there, me.x, me.y, me.c)
+                    landed(ref, self.ss.at[0, 0], self.rs.at[COL, there], me)
+
+                    @pl.when(ahead < me.nz if below else ahead >= 0)
+                    def _():
+                        self.start(ref, ref, TOUP if below else TODOWN, COL, there, me.at(z=ahead))
+                    self.spread(ref, there)
+
+    def neighbours(self):
+        me = self.me
+
+        def event(z):
+            if "x" in self.axes:
+                ref = self.shard(z, 1 - me.x, me.y, me.c)
+                landed(ref, self.ss.at[0, 0], self.rs.at[FROMX, self.key(z)], me)
+                if "y" in self.axes:
+                    half = self.shard(z, 1 - me.x, me.y, me.c, 0)
+                    self.start(half, half, FWDY, DIAGA, z, me.at(y=1 - me.y))
+                self.hand_over(ref, FROMX, z)
+            if "y" in self.axes:
+                ref = self.shard(z, me.x, 1 - me.y, me.c)
+                landed(ref, self.ss.at[0, 0], self.rs.at[FROMY, self.key(z)], me)
+                if "x" in self.axes and self.halves:
+                    half = self.shard(z, me.x, 1 - me.y, me.c, 1)
+                    self.start(half, half, FWDX, DIAGB, z, me.at(x=1 - me.x))
+                self.hand_over(ref, FROMY, z)
+        self.around(event)
+
+    def diagonal(self):
+        me = self.me
+        if "x" not in self.axes or "y" not in self.axes:
+            return
+
+        def event(z):
+            for half in range(2 if self.halves else 1):
+                ref = self.shard(z, 1 - me.x, 1 - me.y, me.c, half)
+                landed(ref, self.ss.at[0, 0], self.rs.at[DIAGA + half, z], me)
+                self.hand_over(ref, DIAGA + half, z)
+        self.around(event)
+
+    def kinds(self):
+        me = self.me
+        found = [(COL, me.x, me.y, None)]
+        if "x" in self.axes:
+            found.append((FROMX, 1 - me.x, me.y, None))
+        if "y" in self.axes:
+            found.append((FROMY, me.x, 1 - me.y, None))
+        if "x" in self.axes and "y" in self.axes:
+            found.append((DIAGA, 1 - me.x, 1 - me.y, 0))
+            if self.halves:
+                found.append((DIAGB, 1 - me.x, 1 - me.y, 1))
+        return found
+
+    def sibling(self):
+        if "c" not in self.axes:
+            return
+        me = self.me
+
+        def event(z):
+            for kind, x, y, half in self.kinds():
+                ref = self.shard(z, x, y, 1 - me.c, half)
+                landed(ref, self.ss.at[0, 0], self.rs.at[5 + kind, self.key(z)], me)
+        self.around(event)
+
+    def drain(self):
+        me = self.me
+
+        def wait(kind, z, half=None):
+            sent(self.shard(z, me.x, me.y, me.c, half), self.ss.at[kind, self.key(z)], self.rs.at[0, 0], me)
+
+        def event(z):
+            if "x" in self.axes:
+                wait(TOX, z)
+            if "y" in self.axes:
+                wait(TOY, z)
+            if "x" in self.axes and "y" in self.axes:
+                wait(FWDY, z, 0)
+                if self.halves:
+                    wait(FWDX, z, 1)
+            if "c" in self.axes:
+                for kind, x, y, half in self.kinds():
+                    wait(TOC + kind, z, half)
+            if "z" in self.axes:
+                pl.when((z <= me.z) & (me.z + 1 < me.nz))(functools.partial(wait, TOUP, z))
+                pl.when((z >= me.z) & (me.z > 0))(functools.partial(wait, TODOWN, z))
+        self.around(event)
+
+    def phases(self):
+        return [self.own, self.column, self.neighbours, self.diagonal, self.sibling, self.drain]
+
+
+def skewed(items):
+    lists = [item.phases() for item in items]
+    for step in range(len(lists) + max(map(len, lists)) - 1):
+        for i, phases in enumerate(lists):
+            if 0 <= step - i < len(phases):
+                phases[step - i]()
+
+
+class Regroup:
+    def __init__(self, me, dp_count, src, dst, ss, rs, width):
+        self.me, self.n, self.src, self.dst, self.ss, self.rs, self.width = me, dp_count, src, dst, ss, rs, width
+
+    def piece(self, dp, y, c):
+        return self.dst.at[dp * 4 + y * 2 + c]
+
+    def columns(self, dp):
+        return self.src.at[:, pl.ds(pl.multiple_of(dp * self.width, 128), self.width)]
+
+    def own(self):
+        me = self.me
+        mine = self.piece(me.dp, me.y, me.c)
+        for k in range(1, self.n):
+            to = lax.rem(me.dp + k, self.n)
+            send(self.columns(to), mine, self.ss.at[0, to], self.rs.at[0, me.dp], (to, me.seq))
+        src = self.columns(me.dp)
+        send(src, mine, self.ss.at[1, me.dp], self.rs.at[1, me.dp], me.at(y=1 - me.y))
+        send(src, mine, self.ss.at[2, me.dp], self.rs.at[2, me.dp], me.at(c=1 - me.c))
+
+    def column(self):
+        me = self.me
+        for k in range(1, self.n):
+            dp = lax.rem(me.dp + k, self.n)
+            ref = self.piece(dp, me.y, me.c)
+            landed(ref, self.ss.at[0, 0], self.rs.at[0, dp], me)
+            send(ref, ref, self.ss.at[1, dp], self.rs.at[1, dp], me.at(y=1 - me.y))
+            send(ref, ref, self.ss.at[2, dp], self.rs.at[2, dp], me.at(c=1 - me.c))
+
+    def neighbours(self):
+        me = self.me
+        for k in range(self.n):
+            dp = lax.rem(me.dp + k, self.n)
+            ref = self.piece(dp, 1 - me.y, me.c)
+            landed(ref, self.ss.at[0, 0], self.rs.at[1, dp], me)
+            send(ref, ref, self.ss.at[3, dp], self.rs.at[3, dp], me.at(c=1 - me.c))
+
+    def sibling(self):
+        me = self.me
+        for dp in range(self.n):
+            landed(self.piece(dp, me.y, 1 - me.c), self.ss.at[0, 0], self.rs.at[2, dp], me)
+            landed(self.piece(dp, 1 - me.y, 1 - me.c), self.ss.at[0, 0], self.rs.at[3, dp], me)
+
+    def drain(self):
+        me = self.me
+        for k in range(self.n):
+            dp = lax.rem(me.dp + k, self.n)
+            ref = self.piece(dp, me.y, me.c)
+            for kind in range(1 if k else 1, 4):
+                sent(ref, self.ss.at[kind, dp], self.rs.at[0, 0], me)
+            if k:
+                sent(ref, self.ss.at[0, dp], self.rs.at[0, 0], me)
+
+    def phases(self):
+        return [self.own, self.column, self.neighbours, self.sibling, self.drain]
+
+
+def gather_kernel(dp_count, plan, *refs):
+    n = len(plan)
+    srcs, dsts = refs[:n], refs[n:2 * n]
+    ss, rs, rss, rrs, local = refs[2 * n:]
+    me = Here(dp_count)
+    greet([me.at(y=1 - me.y), me.at(c=1 - me.c)] + [(lax.rem(me.dp + k, dp_count), me.seq) for k in range(1, dp_count)])
+    items, copies = [], []
+    for i, (axes, halves) in enumerate(plan):
+        if axes == "regroup":
+            item = Regroup(me, dp_count, srcs[i], dsts[i], rss, rrs, halves)
+            copies.append(pltpu.make_async_copy(item.columns(me.dp), item.piece(me.dp, me.y, me.c), local.at[i]))
+        else:
+            item = Gather(me, srcs[i], dsts[i], ss.at[i], rs.at[i], axes, halves)
+            copies.append(pltpu.make_async_copy(srcs[i], item.shard(me.z, me.x, me.y, me.c), local.at[i]))
+        items.append(item)
+    for copy in copies:
+        copy.start()
+    skewed(items)
+    for copy in copies:
+        copy.wait()
+
+
+def gather_all(dp_count, plan, arrays):
+    def out(array, axes, halves):
+        if axes == "regroup":
+            return jax.ShapeDtypeStruct((dp_count * 4, array.shape[0], halves), array.dtype)
+        count = {"zxyc": dp_count * 4, "zx": dp_count, "yc": 4}[axes]
+        return jax.ShapeDtypeStruct((count,) + array.shape, array.dtype)
+    nz = dp_count // 2
+    n = len(plan)
+    return pl.pallas_call(
+        functools.partial(gather_kernel, dp_count, plan),
+        out_shape=tuple(out(a, *p) for a, p in zip(arrays, plan)),
+        in_specs=[ANY] * n,
+        out_specs=tuple([ANY] * n),
+        scratch_shapes=[
+            DMA((n, SEND_KINDS, nz)), DMA((n, RECV_KINDS, nz)),
+            DMA((4, dp_count)), DMA((4, dp_count)), DMA((n,)),
+        ],
+        compiler_params=pltpu.CompilerParams(collective_id=0, has_side_effects=True),
+    )(*arrays)
+
 
 HEADS = 16
 HEAD_DIM = 96
 FRAME_BLOCKS = 2
-
-
 EPS = 1e-05
 NEG = -1e30
 HIGH = lax.Precision.HIGHEST
+F32, BF16 = jnp.float32, jnp.bfloat16
+WIDE = 60 << 20
+PART = 4
+PCOLS = PART * HEAD_DIM
+SCALE = HEAD_DIM ** (-0.5)
+
+
+def dot(left, right):
+    return jnp.dot(left, right, preferred_element_type=F32)
+
+
+def dot_t(left, right):
+    return lax.dot_general(left, right, (((1,), (1,)), ((), ())), preferred_element_type=F32)
+
+
+def t_dot(left, right):
+    return lax.dot_general(left, right, (((0,), (0,)), ((), ())), preferred_element_type=F32)
+
+
+def scaled_rows(rows):
+    mean = jnp.mean(rows, axis=-1, keepdims=True)
+    centred = rows - mean
+    inverse = lax.rsqrt(jnp.mean(centred * centred, axis=-1, keepdims=True) + EPS)
+    return centred * inverse, inverse
+
+
+def norm_back(incoming, scaled, inverse, gain):
+    inner = incoming * gain
+    first = jnp.mean(inner, axis=-1, keepdims=True)
+    second = jnp.mean(inner * scaled, axis=-1, keepdims=True)
+    return inverse * (inner - first - scaled * second)
+
+
+def part_mask(rows):
+    row = lax.broadcasted_iota(jnp.int32, (PART * rows, PCOLS), 0)
+    column = lax.broadcasted_iota(jnp.int32, (PART * rows, PCOLS), 1)
+    low = (row // rows) * HEAD_DIM
+    return (column >= low) & (column < low + HEAD_DIM)
+
+
+def stacked(rows, mask):
+    return jnp.where(mask, jnp.concatenate([rows] * PART, axis=0), jnp.zeros((), rows.dtype))
+
+
+def unstacked(rows, mask, count):
+    kept = jnp.where(mask, rows, 0.0)
+    return sum(kept[h * count:(h + 1) * count] for h in range(PART))
+
+
+def blocks_of(media_rows, block_rows, lat_rows):
+    found = [(b * block_rows, block_rows) for b in range(media_rows // block_rows)]
+    return found + [(media_rows, lat_rows)]
+
+
+def attend_kernel(block_rows, items, owner, media, lat_all, gains, wq, wk, wv,
+                  acc, stats, n_out, nl_out, q_out, k_out, v_out, wbuf, a_ref, m_ref, l_ref, sems):
+    width = media.shape[1]
+    half = width // 2
+    media_rows = media.shape[0]
+    lat_rows = lat_all.shape[0] // items
+    seq = lax.axis_index("seq")
+
+    def fetch(step, slot):
+        cols = pl.ds(pl.multiple_of(step * half, 128), half)
+        return [pltpu.make_async_copy(w.at[:, cols], wbuf.at[slot, i], sems.at[slot, i]) for i, w in enumerate((wq, wk, wv))]
+    for copy in fetch(0, 0):
+        copy.start()
+
+    @pl.loop(0, media_rows // block_rows)
+    def _(b):
+        rows = pl.ds(pl.multiple_of(b * block_rows, block_rows), block_rows)
+        u, _ = scaled_rows(media[rows, :].astype(F32))
+        n_out[rows, :] = (u * gains[2:3, :] + gains[3:4, :]).astype(BF16)
+
+    @pl.loop(0, items)
+    def _(i):
+        rows = pl.ds(pl.multiple_of(i * lat_rows, lat_rows), lat_rows)
+        u, _ = scaled_rows(lat_all[rows, :].astype(F32))
+        nl_out[rows, :] = (u * gains[0:1, :] + gains[1:2, :]).astype(BF16)
+    n_out[pl.ds(media_rows, lat_rows), :] = nl_out[pl.ds(pl.multiple_of(seq * lat_rows, lat_rows), lat_rows), :]
+    stats[...] = jnp.zeros_like(stats)
+    mask = part_mask(lat_rows)
+    lane = lax.broadcasted_iota(jnp.int32, (lat_rows, 128), 1)
+
+    @pl.loop(0, 2)
+    def _(step):
+        slot = lax.rem(step, 2)
+        cols = pl.ds(pl.multiple_of(step * half, 128), half)
+        for copy in fetch(step, slot):
+            copy.wait()
+
+        @pl.when(step == 0)
+        def _():
+            for copy in fetch(1, 1):
+                copy.start()
+        q_out[:, cols] = dot(nl_out[...], wbuf[slot, 0]).astype(BF16)
+        k_out[:, cols] = dot(n_out[...], wbuf[slot, 1]).astype(BF16)
+        v_out[:, cols] = dot(n_out[...], wbuf[slot, 2]).astype(BF16)
+
+        @pl.loop(0, half // PCOLS)
+        def _(inner):
+            part = step * (half // PCOLS) + inner
+            pcols = pl.ds(pl.multiple_of(part * PCOLS, 128), PCOLS)
+            a_ref[...] = jnp.zeros_like(a_ref)
+            l_ref[...] = jnp.zeros_like(l_ref)
+            m_ref[...] = jnp.full_like(m_ref, NEG)
+
+            def block(start, count, item):
+                rows = q_out[pl.ds(pl.multiple_of(item * lat_rows, lat_rows), lat_rows), pcols]
+                query = stacked(rows, mask)
+                keys, values = k_out[pl.ds(start, count), pcols], v_out[pl.ds(start, count), pcols]
+                scores = dot_t(query, keys) * SCALE
+                old = m_ref[item]
+                new = jnp.maximum(old, jnp.max(scores, axis=-1, keepdims=True))
+                factor = jnp.exp(old - new)
+                expo = jnp.exp(scores - new[:, :count])
+                m_ref[item] = new
+                l_ref[item] = l_ref[item] * factor + jnp.sum(expo, axis=-1, keepdims=True)
+                wide = jnp.concatenate([factor] * (PCOLS // 128), axis=1)
+                a_ref[item] = a_ref[item] * wide + dot(expo.astype(BF16), values)
+            for b, (start, count) in enumerate(blocks_of(media_rows, block_rows, lat_rows)):
+                block(start, count, seq if count == lat_rows and start == media_rows else owner[b])
+            for item in range(items):
+                acc[item, :, pcols] = unstacked(a_ref[item], mask, lat_rows).astype(BF16)
+                for h in range(PART):
+                    chosen = lane == part * PART + h
+                    at = pl.ds(h * lat_rows, lat_rows)
+                    stats[item, 0] = jnp.where(chosen, m_ref[item, at, :], stats[item, 0])
+                    stats[item, 1] = jnp.where(chosen, l_ref[item, at, :], stats[item, 1])
+
+
+def attend(owner, media, lat_all, gains, wq, wk, wv, block_rows, items):
+    width = media.shape[1]
+    lat_rows = lat_all.shape[0] // items
+    rows = media.shape[0] + lat_rows
+    shape = jax.ShapeDtypeStruct
+    return pl.pallas_call(
+        functools.partial(attend_kernel, block_rows, items),
+        out_shape=(
+            shape((items, lat_rows, width), BF16), shape((items, 2, lat_rows, 128), F32),
+            shape((rows, width), BF16), shape((items * lat_rows, width), BF16),
+            shape((items * lat_rows, width), BF16), shape((rows, width), BF16), shape((rows, width), BF16),
+        ),
+        in_specs=[pl.BlockSpec(memory_space=pltpu.SMEM), VMEM, VMEM, VMEM, ANY, ANY, ANY],
+        out_specs=tuple([VMEM] * 7),
+        scratch_shapes=[
+            pltpu.VMEM((2, 3, width, width // 2), BF16),
+            pltpu.VMEM((items, PART * lat_rows, PCOLS), F32),
+            pltpu.VMEM((items, PART * lat_rows, 128), F32), pltpu.VMEM((items, PART * lat_rows, 128), F32),
+            DMA((2, 3)),
+        ],
+        compiler_params=pltpu.CompilerParams(vmem_limit_bytes=WIDE),
+    )(owner, media, lat_all, gains, wq, wk, wv)
+
+
+def media_back_kernel(block_rows, items, owner, media, gains, n_ref, nl_ref, q_ref, k_ref, v_ref, do_ref, stats, wq, wk, wv,
+                      gwq, gwk, gwv, media_grad, sums, g_lat,
+                      wbuf, g_ref, gq_ref, dq_acc, dq_ref, dk_ref, dv_ref, sems, out_sem):
+    width = media.shape[1]
+    half = width // 2
+    media_rows = media.shape[0]
+    lat_rows = nl_ref.shape[0] // items
+    seq = lax.axis_index("seq")
+
+    def fetch(step):
+        cols = pl.ds(pl.multiple_of(step * half, 128), half)
+        return [pltpu.make_async_copy(w.at[:, cols], wbuf.at[i], sems.at[i]) for i, w in enumerate((wq, wk, wv))]
+    for copy in fetch(0):
+        copy.start()
+    mask = part_mask(lat_rows)
+    lane = lax.broadcasted_iota(jnp.int32, (lat_rows, 128), 1)
+
+    def replicated(stat, part):
+        pieces = []
+        for h in range(PART):
+            column = jnp.sum(jnp.where(lane == part * PART + h, stat, 0.0), axis=-1, keepdims=True)
+            pieces.append(jnp.broadcast_to(column, (lat_rows, 128)))
+        return jnp.concatenate(pieces, axis=0)
+
+    @pl.loop(0, 2)
+    def _(step):
+        cols = pl.ds(pl.multiple_of(step * half, 128), half)
+
+        @pl.loop(0, half // PCOLS)
+        def _(inner):
+            part = step * (half // PCOLS) + inner
+            pcols = pl.ds(pl.multiple_of(part * PCOLS, 128), PCOLS)
+            lcols = pl.ds(pl.multiple_of(inner * PCOLS, 128), PCOLS)
+            dq_acc[...] = jnp.zeros_like(dq_acc)
+
+            def block(start, count, item):
+                at = pl.ds(pl.multiple_of(item * lat_rows, lat_rows), lat_rows)
+                query, grad = stacked(q_ref[at, pcols], mask), stacked(do_ref[at, pcols], mask)
+                keys, values = k_ref[pl.ds(start, count), pcols], v_ref[pl.ds(start, count), pcols]
+                lse, delta = replicated(stats[item, 0], part), replicated(stats[item, 1], part)
+                prob = jnp.exp(dot_t(query, keys) * SCALE - lse[:, :count])
+                score = (prob * (dot_t(grad, values) - delta[:, :count])).astype(BF16)
+                dq_acc[item] = dq_acc[item] + dot(score, keys)
+                dk_ref[pl.ds(start, count), lcols] = (t_dot(score, query) * SCALE).astype(BF16)
+                dv_ref[pl.ds(start, count), lcols] = t_dot(prob.astype(BF16), grad).astype(BF16)
+            for b, (start, count) in enumerate(blocks_of(media_rows, block_rows, lat_rows)):
+                block(start, count, seq if count == lat_rows and start == media_rows else owner[b])
+            for item in range(items):
+                dq_ref[pl.ds(item * lat_rows, lat_rows), lcols] = (unstacked(dq_acc[item], mask, lat_rows) * SCALE).astype(BF16)
+        for copy in fetch(step):
+            copy.wait()
+        gwq[:, cols] = t_dot(nl_ref[...], dq_ref[...]).astype(BF16)
+        gwk[:, cols] = t_dot(n_ref[...], dk_ref[...]).astype(BF16)
+        gwv[:, cols] = t_dot(n_ref[...], dv_ref[...]).astype(BF16)
+
+        @pl.loop(0, 2)
+        def _(piece):
+            out = pl.ds(pl.multiple_of(piece * half, 128), half)
+            g = dot_t(dk_ref[...], wbuf[1, out, :]) + dot_t(dv_ref[...], wbuf[2, out, :])
+            gq = dot_t(dq_ref[...], wbuf[0, out, :])
+
+            @pl.when(step == 0)
+            def _():
+                g_ref[:, out] = g
+                gq_ref[:, out] = gq
+
+            @pl.when(step == 1)
+            def _():
+                g_ref[:, out] += g
+                gq_ref[:, out] += gq
+
+        @pl.when(step == 0)
+        def _():
+            for copy in fetch(1):
+                copy.start()
+    mine = pl.ds(pl.multiple_of(seq * lat_rows, lat_rows), lat_rows)
+    gq_ref[mine, :] += g_ref[pl.ds(media_rows, lat_rows), :]
+    g_lat[...] = gq_ref[...].astype(BF16)
+    sums[...] = jnp.zeros_like(sums)
+
+    @pl.loop(0, media_rows // block_rows)
+    def _(b):
+        rows = pl.ds(pl.multiple_of(b * block_rows, block_rows), block_rows)
+        u, inverse = scaled_rows(media[rows, :].astype(F32))
+        g = g_ref[rows, :]
+        g_ref[rows, :] = norm_back(g, u, inverse, gains[2:3, :])
+        pltpu.make_async_copy(g_ref.at[rows, :], media_grad.at[rows, :], out_sem).start()
+        sums[0:1, :] += jnp.sum(g * u, axis=0, keepdims=True)
+        sums[1:2, :] += jnp.sum(g, axis=0, keepdims=True)
+    whole = pl.ds(0, media_rows)
+    pltpu.make_async_copy(g_ref.at[whole, :], media_grad.at[whole, :], out_sem).wait()
+
+
+def media_back(owner, media, gains, n, nl, q, k, v, do_all, stats, wq, wk, wv, block_rows, items):
+    width = media.shape[1]
+    half = width // 2
+    lat_rows = nl.shape[0] // items
+    rows = n.shape[0]
+    shape = jax.ShapeDtypeStruct
+    return pl.pallas_call(
+        functools.partial(media_back_kernel, block_rows, items),
+        out_shape=(
+            shape((width, width), BF16), shape((width, width), BF16), shape((width, width), BF16),
+            shape(media.shape, F32), shape((8, width), F32), shape((items * lat_rows, width), BF16),
+        ),
+        in_specs=[pl.BlockSpec(memory_space=pltpu.SMEM)] + [VMEM] * 9 + [ANY] * 3,
+        out_specs=(VMEM, VMEM, VMEM, ANY, VMEM, VMEM),
+        scratch_shapes=[
+            pltpu.VMEM((3, width, half), BF16),
+            pltpu.VMEM((rows, width), F32), pltpu.VMEM((items * lat_rows, width), F32),
+            pltpu.VMEM((items, PART * lat_rows, PCOLS), F32),
+            pltpu.VMEM((items * lat_rows, half), BF16), pltpu.VMEM((rows, half), BF16), pltpu.VMEM((rows, half), BF16),
+            DMA((3,)), DMA,
+        ],
+        compiler_params=pltpu.CompilerParams(vmem_limit_bytes=WIDE),
+    )(owner, media, gains, n, nl, q, k, v, do_all, stats, wq, wk, wv)
+
+
+def dp_peers(me, dp_count):
+    return [(lax.rem(me.dp + k, dp_count), me.seq) for k in range(1, dp_count)]
+
+
+def far_first(me, event):
+    for d in range(me.nz - 1, 0, -1):
+        pl.when(me.z >= d)(functools.partial(event, me.z - d))
+        pl.when(me.z + d < me.nz)(functools.partial(event, me.z + d))
+    event(me.z)
+
+
+def add(*refs):
+    total = refs[0][...].astype(F32)
+    for ref in refs[1:]:
+        total = total + ref[...].astype(F32)
+    return total
+
+
+class Line:
+    def __init__(self, me, column, from_below, from_above, ss, rs):
+        self.me, self.column, self.zb, self.za, self.ss, self.rs = me, column, from_below, from_above, ss, rs
+
+    def event(self, z):
+        me = self.me
+        for up in (True, False):
+            buf, kind = (self.zb, 0) if up else (self.za, 1)
+            first = me.z == 0 if up else me.z == me.nz - 1
+            to = me.at(z=me.z + 1 if up else me.z - 1)
+
+            @pl.when(z > me.z if up else z < me.z)
+            def _():
+                term = self.column(z)
+
+                @pl.when(jnp.logical_not(first))
+                def _():
+                    landed(buf.at[z], self.ss.at[0, 0], self.rs.at[kind, z], me)
+                    term[...] = add(term, buf.at[z]).astype(term.dtype)
+                send(term, buf.at[z], self.ss.at[kind, z], self.rs.at[kind, z], to)
+
+    def total(self, out):
+        me = self.me
+        out[...] = self.column(me.z)[...].astype(F32)
+        for up in (True, False):
+            buf, kind = (self.zb, 0) if up else (self.za, 1)
+
+            @pl.when(me.z > 0 if up else me.z < me.nz - 1)
+            def _():
+                landed(buf.at[me.z], self.ss.at[0, 0], self.rs.at[kind, me.z], me)
+                out[...] += buf.at[me.z][...].astype(F32)
+
+    def drain(self):
+        me = self.me
+
+        def event(z):
+            pl.when(z > me.z)(lambda: sent(self.zb.at[z], self.ss.at[0, z], self.rs.at[0, 0], me))
+            pl.when(z < me.z)(lambda: sent(self.za.at[z], self.ss.at[1, z], self.rs.at[0, 0], me))
+        far_first(me, event)
+
+
+class DpScatter:
+    def __init__(self, me, part, out, ox, zb, za, ss, rs):
+        self.me, self.part, self.out, self.ox, self.ss, self.rs = me, part, out, ox, ss, rs
+        self.line = Line(me, lambda z: part.at[z * 2 + me.x], zb, za, ss, rs)
+
+    def start(self, z):
+        me = self.me
+        send(self.part.at[z * 2 + 1 - me.x], self.ox.at[z], self.ss.at[2, z], self.rs.at[2, z], me.at(x=1 - me.x))
+
+    def fold(self, z):
+        me = self.me
+        landed(self.ox.at[z], self.ss.at[0, 0], self.rs.at[2, z], me)
+        mine = self.part.at[z * 2 + me.x]
+        mine[...] = add(mine, self.ox.at[z]).astype(mine.dtype)
+        self.line.event(z)
+
+    def finish(self):
+        self.line.total(self.out)
+
+    def drain(self):
+        far_first(self.me, lambda z: sent(self.ox.at[z], self.ss.at[2, z], self.rs.at[0, 0], self.me))
+        self.line.drain()
+
+
+def head_columns(width):
+    row = lax.broadcasted_iota(jnp.int32, (128, width), 0) * HEAD_DIM
+    column = lax.broadcasted_iota(jnp.int32, (128, width), 1)
+    return ((column >= row) & (column < row + HEAD_DIM)).astype(F32)
+
+
+def exact(left, right):
+    return jnp.dot(left, right, preferred_element_type=F32, precision=HIGH)
+
+
+def exact_t(left, right):
+    return lax.dot_general(left, right, (((1,), (1,)), ((), ())), preferred_element_type=F32, precision=HIGH)
+
+
+def latent_kernel(dp_count, acc, stats, lat, gains, og_all, wo, wup, wdn,
+                  lat_out, grad_hidden, do_all, stat_all, gwo, gwu, gwd, sums,
+                  acc_in, stat_in, nf_all, og, wo_v, up_v, dn_v, ga, act, gp,
+                  part_g, ox_g, zb_g, za_g, part_y, ox_y, zb_y, za_y, own_do, own_stat, row_a, row_b, do_in, st_in,
+                  xs, xr, ls, gs, gr, gs2, gr2, gs3, gr3, ys, yr, ws, wr):
+    me = Here(dp_count)
+    seq_count = acc.shape[0]
+    rows, width = lat.shape
+    seq_peers = [lax.rem(me.seq + k, seq_count) for k in range(1, seq_count)]
+    loads = [pltpu.make_async_copy(src, dst, ls.at[i]) for i, (src, dst) in enumerate(((wdn, dn_v), (og_all, og), (wo, wo_v), (wup, up_v)))]
+    for load in loads:
+        load.start()
+    greet(dp_peers(me, dp_count) + [(me.dp, s) for s in seq_peers])
+    for k, to in enumerate(seq_peers):
+        send(acc.at[to], acc_in.at[me.seq], xs.at[0, k], xr.at[0, me.seq], (me.dp, to))
+        send(stats.at[to], stat_in.at[me.seq], xs.at[1, k], xr.at[1, me.seq], (me.dp, to))
+    acc_in[me.seq] = acc[me.seq]
+    stat_in[me.seq] = stats[me.seq]
+    loads[0].wait()
+    loads[1].wait()
+    hidden_cols = dn_v.shape[0]
+    all_rows = dp_count * rows
+
+    @pl.loop(0, hidden_cols // 256)
+    def _(t):
+        at = pl.ds(pl.multiple_of(t * 256, 256), 256)
+        ga[:, at] = dot_t(og[...].reshape(all_rows, width), dn_v[at, :])
+    for k, source in enumerate(seq_peers):
+        landed(acc_in.at[source], xs.at[0, 0], xr.at[0, source], me)
+        landed(stat_in.at[source], xs.at[0, 0], xr.at[1, source], me)
+    tops = [stat_in[s, 0] for s in range(seq_count)]
+    best = functools.reduce(jnp.maximum, tops)
+    weights = [jnp.exp(top - best) for top in tops]
+    total = sum(w * stat_in[s, 1] for s, w in enumerate(weights))
+    lane = lax.broadcasted_iota(jnp.int32, total.shape, 1)
+    total = jnp.where(lane < HEADS, total, 1.0)
+    spread = head_columns(width)
+    attended = sum(exact(w / total, spread) * acc_in[s].astype(F32) for s, w in enumerate(weights))
+    row_a[...] = attended
+    own_stat[0] = best + jnp.log(total)
+    loads[2].wait()
+    loads[3].wait()
+    hidden = lat[...].astype(F32) + dot(attended.astype(BF16), wo_v[...])
+    row_b[...] = hidden
+    scaled, _ = scaled_rows(hidden)
+    nf_all[me.dp] = (scaled * gains[4:5, :] + gains[5:6, :]).astype(BF16)
+    spread_nf = Gather(me, nf_all.at[me.dp], nf_all, gs, gr, "zx", 0)
+    spread_nf.own()
+    spread_nf.column()
+    spread_nf.neighbours()
+
+    @pl.loop(0, hidden_cols // 256)
+    def _(t):
+        at = pl.ds(pl.multiple_of(t * 256, 256), 256)
+        pre = dot(nf_all[...].reshape(all_rows, width), up_v[:, at])
+        phi = 0.5 * (1.0 + lax.erf(pre * 0.7071067811865476))
+        act[:, at] = (pre * phi).astype(BF16)
+        slope = phi + pre * jnp.exp(pre * pre * -0.5) * 0.3989422804014327
+        gp[:, at] = (ga[:, at] * slope).astype(BF16)
+
+    @pl.loop(0, width // 512)
+    def _(t):
+        at = pl.ds(pl.multiple_of(t * 512, 512), 512)
+        part_g[:, :, at] = dot_t(gp[...], up_v[at, :]).astype(BF16).reshape(dp_count, rows, 512)
+    sum_g = DpScatter(me, part_g, own_do, ox_g, zb_g, za_g, gs2, gr2)
+    far_first(me, sum_g.start)
+
+    @pl.loop(0, width // 512)
+    def _(t):
+        at = pl.ds(pl.multiple_of(t * 512, 512), 512)
+        part_y[:, :, at] = dot(act[...], dn_v[:, at]).astype(BF16).reshape(dp_count, rows, 512)
+    far_first(me, sum_g.fold)
+    sum_y = DpScatter(me, part_y, own_do, ox_y, zb_y, za_y, gs3, gr3)
+    far_first(me, sum_y.start)
+    gwd[...] = t_dot(act[...], og[...].reshape(all_rows, width)).astype(BF16)
+    sum_g.finish()
+    gathered = own_do[...]
+    scaled, inverse = scaled_rows(row_b[...])
+    sums[...] = jnp.zeros_like(sums)
+    sums[0:1, :] = jnp.sum(gathered * scaled, axis=0, keepdims=True)
+    sums[1:2, :] = jnp.sum(gathered, axis=0, keepdims=True)
+    grad = og[me.dp].astype(F32) + norm_back(gathered, scaled, inverse, gains[4:5, :])
+    grad_hidden[...] = grad
+    low = grad.astype(BF16)
+    grad_att = dot_t(low, wo_v[...]).astype(BF16)
+    do_in[me.seq] = grad_att
+    own_stat[1] = exact_t(grad_att.astype(F32) * row_a[...], spread)
+    st_in[me.seq] = own_stat[...]
+    spread_do = Gather(me, do_in.at[me.seq], do_in, ys, yr, "yc", 0)
+    spread_st = Gather(me, st_in.at[me.seq], st_in, ws, wr, "yc", 0)
+    spread_do.own()
+    spread_st.own()
+    far_first(me, sum_y.fold)
+    gwo[...] = t_dot(row_a[...].astype(BF16), low).astype(BF16)
+    spread_do.neighbours()
+    spread_st.neighbours()
+    gwu[...] = t_dot(nf_all[...].reshape(all_rows, width), gp[...]).astype(BF16)
+    sum_y.finish()
+    lat_out[...] = (row_b[...] + own_do[...]).astype(BF16)
+    spread_do.sibling()
+    spread_st.sibling()
+    do_all[...] = do_in[...]
+    stat_all[...] = st_in[...]
+    for k, to in enumerate(seq_peers):
+        sent(acc_in.at[0], xs.at[0, k], xr.at[0, 0], me)
+        sent(stat_in.at[0], xs.at[1, k], xr.at[0, 0], me)
+    for item in (spread_nf, sum_g, sum_y, spread_do, spread_st):
+        item.drain()
+
+
+def latent(dp_count, acc, stats, lat, gains, og_all, wo, wup, wdn):
+    nz = dp_count // 2
+    items, rows, width = acc.shape
+    hidden = wdn.shape[0]
+    shape = jax.ShapeDtypeStruct
+    buf = lambda *s: pltpu.VMEM(s, BF16)
+    all_rows = dp_count * rows
+    gather_sems = [DMA((SEND_KINDS, nz)), DMA((RECV_KINDS, nz))]
+    return pl.pallas_call(
+        functools.partial(latent_kernel, dp_count),
+        out_shape=(
+            shape((rows, width), BF16), shape((rows, width), F32), shape((items, rows, width), BF16),
+            shape((items, 2, rows, 128), F32), shape((width, width), BF16), shape((width, hidden), BF16),
+            shape((hidden, width), BF16), shape((8, width), F32),
+        ),
+        in_specs=[VMEM] * 4 + [ANY] * 4,
+        out_specs=tuple([VMEM] * 8),
+        scratch_shapes=[
+            buf(items, rows, width), pltpu.VMEM((items, 2, rows, 128), F32), buf(dp_count, rows, width), buf(dp_count, rows, width),
+            buf(width, width), buf(width, hidden), buf(hidden, width),
+            pltpu.VMEM((all_rows, hidden), F32), buf(all_rows, hidden), buf(all_rows, hidden),
+            buf(dp_count, rows, width), buf(nz, rows, width), buf(nz, rows, width), buf(nz, rows, width),
+            buf(dp_count, rows, width), buf(nz, rows, width), buf(nz, rows, width), buf(nz, rows, width),
+            pltpu.VMEM((rows, width), F32), pltpu.VMEM((2, rows, 128), F32),
+            pltpu.VMEM((rows, width), F32), pltpu.VMEM((rows, width), F32),
+            buf(items, rows, width), pltpu.VMEM((items, 2, rows, 128), F32),
+            DMA((2, items)), DMA((2, items)), DMA((4,)),
+            *gather_sems, DMA((3, nz)), DMA((3, nz)), DMA((3, nz)), DMA((3, nz)), *gather_sems, *gather_sems,
+        ],
+        compiler_params=pltpu.CompilerParams(collective_id=1, has_side_effects=True, vmem_limit_bytes=WIDE),
+    )(acc, stats, lat, gains, og_all, wo, wup, wdn)
+
+
+class Scatter:
+    def __init__(self, me, src, out, bufs, ss, rs, ls, lss, lrs):
+        self.me, self.src, self.out, self.ss, self.rs, self.ls = me, src, out, ss, rs, ls
+        self.acc, self.cbuf, self.x1, self.y1, self.ox, self.oy, zb, za = bufs
+        self.half = src.shape[-1] // 2
+        self.line = Line(me, lambda z: self.acc.at[z, me.x, me.y], zb, za, lss, lrs)
+
+    def part(self, ref, half):
+        return ref.at[:, pl.ds(half * self.half, self.half)]
+
+    def load(self, z):
+        return pltpu.make_async_copy(self.src.at[pl.ds(2 * z, 2), :, self.me.c], self.acc.at[z], self.ls.at[z])
+
+    def begin(self):
+        me = self.me
+
+        def event(z):
+            send(self.src.at[pl.ds(2 * z, 2), :, 1 - me.c], self.cbuf.at[z], self.ss.at[0, z], self.rs.at[0, z], me.at(c=1 - me.c))
+            self.load(z).start()
+        far_first(me, event)
+
+    def core(self):
+        me = self.me
+
+        def event(z):
+            self.load(z).wait()
+            landed(self.cbuf.at[z], self.ss.at[0, 0], self.rs.at[0, z], me)
+            mine = self.acc.at[z]
+
+            @pl.loop(0, 4)
+            def _(i):
+                x, y = i // 2, i % 2
+                mine[x, y] = (mine[x, y].astype(F32) + self.cbuf[z, x, y].astype(F32)).astype(BF16)
+            x_to, y_to = me.at(x=1 - me.x), me.at(y=1 - me.y)
+            diag = mine.at[1 - me.x, 1 - me.y]
+            send(self.part(diag, 0), self.x1.at[z], self.ss.at[1, z], self.rs.at[1, z], x_to)
+            send(self.part(diag, 1), self.y1.at[z], self.ss.at[2, z], self.rs.at[2, z], y_to)
+            send(self.part(mine.at[1 - me.x, me.y], 0), self.part(self.ox.at[z], 0), self.ss.at[3, z], self.rs.at[3, z], x_to)
+            send(self.part(mine.at[me.x, 1 - me.y], 1), self.part(self.oy.at[z], 1), self.ss.at[4, z], self.rs.at[4, z], y_to)
+        far_first(me, event)
+
+    def middle(self):
+        me = self.me
+
+        def event(z):
+            landed(self.x1.at[z], self.ss.at[0, 0], self.rs.at[1, z], me)
+            ref = self.part(self.acc.at[z, me.x, 1 - me.y], 0)
+            ref[...] = add(ref, self.x1.at[z]).astype(BF16)
+            send(ref, self.part(self.oy.at[z], 0), self.ss.at[5, z], self.rs.at[5, z], me.at(y=1 - me.y))
+            landed(self.y1.at[z], self.ss.at[0, 0], self.rs.at[2, z], me)
+            ref = self.part(self.acc.at[z, 1 - me.x, me.y], 1)
+            ref[...] = add(ref, self.y1.at[z]).astype(BF16)
+            send(ref, self.part(self.ox.at[z], 1), self.ss.at[6, z], self.rs.at[6, z], me.at(x=1 - me.x))
+        far_first(me, event)
+
+    def fold(self):
+        me = self.me
+
+        def event(z):
+            for kind, ref in ((3, self.part(self.ox.at[z], 0)), (4, self.part(self.oy.at[z], 1)),
+                              (5, self.part(self.oy.at[z], 0)), (6, self.part(self.ox.at[z], 1))):
+                landed(ref, self.ss.at[0, 0], self.rs.at[kind, z], me)
+            mine = self.acc.at[z, me.x, me.y]
+            mine[...] = add(mine, self.ox.at[z], self.oy.at[z]).astype(BF16)
+            self.line.event(z)
+        far_first(me, event)
+
+    def finish(self):
+        self.line.total(self.out)
+
+    def drain(self):
+        me = self.me
+
+        def event(z):
+            sent(self.cbuf.at[z], self.ss.at[0, z], self.rs.at[0, 0], me)
+            for kind in range(1, 7):
+                sent(self.x1.at[z], self.ss.at[kind, z], self.rs.at[0, 0], me)
+        far_first(me, event)
+        self.line.drain()
+
+    def phases(self):
+        return [self.begin, self.core, self.middle, self.fold, self.finish, self.drain]
+
+    @staticmethod
+    def scratch(nz, rows, cols):
+        buf = lambda *s: pltpu.VMEM(s + (rows, cols), BF16)
+        half = pltpu.VMEM((nz, rows, cols // 2), BF16)
+        return [buf(nz, 2, 2), buf(nz, 2, 2), half, half, buf(nz), buf(nz), buf(nz), buf(nz),
+                DMA((7, nz)), DMA((7, nz)), DMA((nz,)), DMA((2, nz)), DMA((2, nz))]
+
+
+class SeqScatter:
+    def __init__(self, me, src, then, acc, cbuf, oy, ss, rs, ls):
+        self.me, self.src, self.then, self.acc, self.cbuf, self.oy = me, src, then, acc, cbuf, oy
+        self.ss, self.rs = ss, rs
+        self.load = pltpu.make_async_copy(src.at[:, :, me.c], acc, ls.at[0])
+
+    def begin(self):
+        me = self.me
+        send(self.src.at[:, :, 1 - me.c], self.cbuf, self.ss.at[0], self.rs.at[0], me.at(c=1 - me.c))
+        self.load.start()
+
+    def core(self):
+        me = self.me
+        self.load.wait()
+        landed(self.cbuf, self.ss.at[0], self.rs.at[0], me)
+
+        @pl.loop(0, self.acc.shape[0])
+        def _(i):
+            for y in (0, 1):
+                self.acc[i, y] = (self.acc[i, y].astype(F32) + self.cbuf[i, y].astype(F32)).astype(BF16)
+        send(self.acc.at[:, 1 - me.y], self.oy, self.ss.at[1], self.rs.at[1], me.at(y=1 - me.y))
+
+    def fold(self):
+        me = self.me
+        landed(self.oy, self.ss.at[0], self.rs.at[1], me)
+
+        @pl.loop(0, self.acc.shape[0])
+        def _(i):
+            self.oy[i] = (self.acc[i, me.y].astype(F32) + self.oy[i].astype(F32)).astype(BF16)
+
+    def finish(self):
+        self.then(self.oy)
+
+    def drain(self):
+        sent(self.cbuf, self.ss.at[0], self.rs.at[0], self.me)
+        sent(self.oy, self.ss.at[1], self.rs.at[0], self.me)
+
+    def phases(self):
+        return [self.begin, self.core, self.fold, self.finish, self.drain]
+
+    @staticmethod
+    def scratch(count, rows, cols):
+        buf = lambda *s: pltpu.VMEM(s + (rows, cols), BF16)
+        return [buf(count, 2), buf(count, 2), buf(count), DMA((2,)), DMA((2,)), DMA((1,))]
+
+
+class SumAll:
+    def __init__(self, me, ref, inbox, ss, rs):
+        self.me, self.ref, self.inbox, self.ss, self.rs = me, ref, inbox, ss, rs
+
+    def step(self, i, to):
+        def begin():
+            send(self.ref.at[i], self.inbox.at[i], self.ss.at[i], self.rs.at[i], to)
+
+        def end():
+            landed(self.inbox.at[i], self.ss.at[0], self.rs.at[i], self.me)
+            self.ref[i + 1] = self.ref[i] + self.inbox[i]
+        return begin, end
+
+    def phases(self):
+        me = self.me
+        n = me.nz
+
+        def begin_z():
+            for k in range(1, n):
+                to = lax.rem(me.z + k, n)
+                send(self.ref.at[3], self.inbox.at[2 + k], self.ss.at[2 + k], self.rs.at[2 + k], me.at(z=to))
+
+        def end_z():
+            total = self.ref[3]
+            for k in range(1, n):
+                landed(self.inbox.at[2 + k], self.ss.at[0], self.rs.at[2 + k], me)
+                total = total + self.inbox[2 + k]
+            self.ref[4] = total
+
+        def drain():
+            for i in range(2 + n):
+                sent(self.ref.at[0], self.ss.at[i], self.rs.at[0], me)
+        first = self.step(0, me.at(c=1 - me.c))
+        second = self.step(1, me.at(x=1 - me.x))
+        third = self.step(2, me.at(y=1 - me.y))
+        both = lambda one, other: (lambda: (one(), other()))
+        return [first[0], both(first[1], second[0]), both(second[1], third[0]), both(third[1], begin_z), end_z, drain]
+
+
+def scatter_kernel(dp_count, *refs):
+    me = Here(dp_count)
+    (g_lat, lat, grad_hidden, gains, sums_media, sums_ffn, gwq, gwk, gwv, gwo, gwu, gwd) = refs[:12]
+    (lat_grad, sums, out_q, out_k, out_v, out_o, out_up, out_dn) = refs[12:20]
+    scratch = list(refs[20:])
+    take = lambda n: [scratch.pop(0) for _ in range(n)]
+    full = [take(13) for _ in range(4)]
+    seqs = [take(6) for _ in range(3)]
+    up_in, up_ss, up_rs = take(3)
+    small = take(4)
+    greet(dp_peers(me, dp_count) + [me.at(y=1 - me.y), me.at(c=1 - me.c)])
+    all_sum = SumAll(me, *small)
+
+    def latents(total):
+        scaled, inverse = scaled_rows(lat[...].astype(F32))
+        grad = total[0].astype(F32)
+        lat_grad[...] = grad_hidden[...] + norm_back(grad, scaled, inverse, gains[0:1, :])
+        first = small[0]
+        first[0, 0:1, :] = jnp.sum(grad * scaled, axis=0, keepdims=True)
+        first[0, 1:2, :] = jnp.sum(grad, axis=0, keepdims=True)
+        first[0, 2:4, :] = sums_media[0:2, :]
+        first[0, 4:6, :] = sums_ffn[0:2, :]
+        first[0, 6:8, :] = jnp.zeros_like(sums_ffn[0:2, :])
+
+    def down(total):
+        out_dn[...] = total[0].astype(F32)
+
+    def up(total):
+        for k in range(1, dp_count):
+            to = lax.rem(me.dp + k, dp_count)
+            send(total.at[to], up_in.at[me.dp], up_ss.at[to], up_rs.at[me.dp], (to, me.seq))
+        up_in[me.dp] = total[me.dp]
+
+    class Up(SeqScatter):
+        def collect(self):
+            for dp in range(dp_count):
+                pl.when(dp != me.dp)(lambda: landed(up_in.at[dp], up_ss.at[0], up_rs.at[dp], me))
+                cols = up_in.shape[2]
+                out_up[:, dp * cols:(dp + 1) * cols] = up_in[dp].astype(F32)
+
+        def drain(self):
+            super().drain()
+            for k in range(1, dp_count):
+                to = lax.rem(me.dp + k, dp_count)
+                sent(up_in.at[0], up_ss.at[to], up_rs.at[0], me)
+
+        def phases(self):
+            return [self.begin, self.core, self.fold, self.finish, self.collect, self.drain]
+    lat_item = SeqScatter(me, g_lat, latents, *seqs[0])
+    up_item = Up(me, gwu, up, *seqs[1])
+    down_item = SeqScatter(me, gwd, down, *seqs[2])
+    fulls = [Scatter(me, src, out, f[:8], *f[8:]) for src, out, f in zip((gwo, gwv, gwk, gwq), (out_o, out_v, out_k, out_q), full)]
+
+    class After:
+        def phases(self):
+            return all_sum.phases()
+    skewed([lat_item, fulls[0], up_item, After(), fulls[1], down_item, fulls[2], fulls[3]])
+    sums[...] = small[0][4]
+
+
+def scatter_all(dp_count, g_lat, lat, grad_hidden, gains, sums_media, sums_ffn, gwq, gwk, gwv, gwo, gwu, gwd):
+    nz = dp_count // 2
+    rows, width = lat.shape
+    hidden = gwu.shape[1]
+    n = dp_count * 4
+    shape = jax.ShapeDtypeStruct
+    square = lambda g: g.reshape(dp_count, 2, 2, width // n, width)
+    arrays = (
+        g_lat.reshape(1, 2, 2, rows, width), lat, grad_hidden, gains, sums_media, sums_ffn,
+        square(gwq), square(gwk), square(gwv), square(gwo),
+        gwu.reshape(dp_count, 2, 2, width // n, hidden), gwd.reshape(1, 2, 2, hidden // 4, width),
+    )
+    return pl.pallas_call(
+        functools.partial(scatter_kernel, dp_count),
+        out_shape=(
+            shape((rows, width), F32), shape((8, width), F32),
+            *[shape((width // n, width), F32)] * 4, shape((width // n, hidden * dp_count), F32), shape((hidden // 4, width), F32),
+        ),
+        in_specs=[ANY] + [VMEM] * 5 + [ANY] * 6,
+        out_specs=tuple([VMEM] * 8),
+        scratch_shapes=[
+            *(Scatter.scratch(nz, width // n, width) * 4),
+            *SeqScatter.scratch(1, rows, width), *SeqScatter.scratch(dp_count, width // n, hidden), *SeqScatter.scratch(1, hidden // 4, width),
+            pltpu.VMEM((dp_count, width // n, hidden), BF16), DMA((dp_count,)), DMA((dp_count,)),
+            pltpu.VMEM((5, 8, width), F32), pltpu.VMEM((2 + nz, 8, width), F32), DMA((2 + nz,)), DMA((2 + nz,)),
+        ],
+        compiler_params=pltpu.CompilerParams(collective_id=2, has_side_effects=True, vmem_limit_bytes=WIDE),
+    )(*arrays)
+
+
+def local_fast(
+    media, latents, out_grad, frame_counts, block_position, w_query, w_key, w_value, w_out, w_up, w_down,
+    gain_lat, shift_lat, gain_media, shift_media, gain_ffn, shift_ffn,
+):
+    dp_count, seq_count = lax.axis_size("dp"), lax.axis_size("seq")
+    seq = lax.axis_index("seq")
+    blocks, block_rows, width = media.shape
+    items, lat_rows = seq_count, latents.shape[1]
+    own_cols = gain_lat.shape[0]
+    ends = FRAME_BLOCKS * jnp.cumsum(frame_counts[0])
+    position = lax.dynamic_slice_in_dim(block_position[0], seq * blocks, blocks)
+    owner = jnp.sum((ends[None, :] <= position[:, None]).astype(jnp.int32), axis=1)
+    vectors = jnp.stack([gain_lat, shift_lat, gain_media, shift_media, gain_ffn, shift_ffn]).astype(F32)
+    pack = jnp.pad(vectors, ((0, 2), (0, 128 - own_cols)))
+    lat, og = latents.reshape(lat_rows, width), out_grad.reshape(lat_rows, width)
+    plan = [("zxyc", 0), ("yc", 0)] + [("zxyc", width // 2)] * 4 + [("zx", 0), ("yc", 0), ("regroup", w_up.shape[1] // dp_count)]
+    packs, lat_all, wq, wk, wv, wo, og_all, wdn, wup = gather_all(
+        dp_count, plan, (pack, lat, w_query, w_key, w_value, w_out, og, w_down, w_up))
+    gains = jnp.swapaxes(packs[:, :, :own_cols], 0, 1).reshape(8, width)
+    wq, wk, wv, wo = [w.reshape(width, width) for w in (wq, wk, wv, wo)]
+    wdn, wup = wdn.reshape(-1, width), wup.reshape(width, -1)
+    med = media.reshape(-1, width)
+    acc, stats, n, nl, q, k, v = attend(owner, med, lat_all.reshape(-1, width), gains, wq, wk, wv, block_rows, items)
+    lat_out, grad_hidden, do_all, stat_all, gwo, gwu, gwd, sums_ffn = latent(dp_count, acc, stats, lat, gains, og_all, wo, wup, wdn)
+    gwq, gwk, gwv, media_grad, sums_media, g_lat = media_back(
+        owner, med, gains, n, nl, q, k, v, do_all.reshape(-1, width), stat_all, wq, wk, wv, block_rows, items)
+    lat_grad, sums, *grads = scatter_all(
+        dp_count, g_lat, lat, grad_hidden, gains, sums_media, sums_ffn, gwq, gwk, gwv, gwo, gwu, gwd)
+    place = (lax.axis_index("dp") * seq_count + seq) * own_cols
+    own = lax.dynamic_slice_in_dim(sums, place, own_cols, axis=1)
+    return (lat_out.reshape(latents.shape), lat_grad.reshape(latents.shape), media_grad.reshape(media.shape), *grads, *[own[i] for i in range(6)])
+
+
+def fits(mesh):
+    return mesh.shape["seq"] == 4 and mesh.shape["dp"] % 2 == 0 and 1536 % (mesh.shape["dp"] * 64) == 0
 
 
 def norm_forward(rows, gain, shift):
@@ -363,7 +1502,7 @@
 
 def solution(mesh):
     return jax.shard_map(
-        local,
+        local_fast if fits(mesh) else local,
         mesh=mesh,
         in_specs=(
             P(("dp", "seq"), None, None),

time: 1920 us -> 476 us (0.25)
  waiting for transfers between devices: 1420 us -> 0 us
  Pallas kernels: 0 us -> 453 us
  matrix products: 211 us -> 0 us
  blocking collectives: 120 us -> 0 us
  local copies, waits for them, and re-layouts: 102 us -> 14 us
  other arithmetic: 25.8 us -> 2.02 us
    reduce_scatter x7 -> x0, waiting for transfers between devices: 1110 us -> none  [the longest x1 355 us: local(): lax.psum_scatter(grad_up, ('dp', 'seq'), scatter_dimension=0, tiled=True)]
    pallas_call x0 -> x5, Pallas kernels: none -> 453 us  [the longest x1 138 us: gather_all(): pl.pallas_call(functools.partial(gather_kernel, dp_count, plan), out_shap...]
    all_gather x6 -> x0, waiting for transfers between devices: 307 us -> none  [the longest x1 114 us: local(): lax.all_gather(w_down, ('dp', 'seq'), axis=0, tiled=True)]
    dot_general x39 -> x0, matrix products: 211 us -> none  [the longest x8 66.6 us: matmul_left_t(): lax.dot_general(left, right, (((0,), (0,)), ((), ())), preferred_element_...]
    unnamed x2 -> x0, blocking collectives: 81.8 us -> none
    reshape x13 -> x1, local copies, waits for them, and re-layouts: 45.2 us -> 0.73 us  [local_fast(): gains = jnp.swapaxes(packs[:, :, :own_cols], 0, 1).reshape(8, width)]
    all_gather x5 -> x0, blocking collectives: 38.3 us -> none  [the longest x1 10.7 us: local(): lax.all_gather(grad_att.reshape(local_items, lat_rows, width), 'seq', axi...]
  transfers between devices with their start and end apart: 16 -> 0, of which waited for: 10 -> 0; matrix products, arithmetic and copies ran while one was open for 14% -> 0% of each run, Pallas kernels for 0% -> 0%
where the time goes in v1:
time: 476 us; the launch traced here: 470 us
  Pallas kernels  453 us (95%)
  local copies, waits for them, and re-layouts  14 us (3%)
    pallas_call x1, Pallas kernels, gather_all(): pl.pallas_call(functools.partial(gather_kernel, dp_count, plan), out_shap...  138 us
    pallas_call x1, Pallas kernels, scatter_all(): pl.pallas_call(functools.partial(scatter_kernel, dp_count), out_shape=(sh...  137 us
    pallas_call x1, Pallas kernels, latent(): pl.pallas_call(functools.partial(latent_kernel, dp_count), out_shape=(sha...  100 us
    pallas_call x1, Pallas kernels, media_back(): pl.pallas_call(functools.partial(media_back_kernel, block_rows, items), o...  48.9 us
    pallas_call x1, Pallas kernels, attend(): pl.pallas_call(functools.partial(attend_kernel, block_rows, items), out_s...  29.3 us
    unnamed x22, local copies, waits for them, and re-layouts  10.1 us

profile of v1, /device:TPU:0, one launch (start us, length us, event | category | flops | bytes accessed | tf_op | source)
XLA Modules:
  0.0 470.0 jit_solution(12930361764229944591)
XLA Ops:
  0.6 0.0 copy-start
  0.7 0.6 copy-done
  1.3 0.1 dynamic-slice_bitcast_fusion
  1.4 0.8 reduce-window.8
  2.2 0.6 convert_reduce_fusion.owner
  2.8 0.8 stack.27
  3.6 0.6 pad_convert_fusion.refs_0_
  4.2 138.0 %shard_map.280 = (f32[32,8,128]{2,1,0:T(8,128)}, bf16[4,64,1536]{2,1,0:T(8,128)(2,1)}, bf16[32,48,1536]{2,1,0:T(8,128)(2,1)}, bf16[32,48,1536]{2,1,0:T(8,128)(2,...) custom-call(f32[8,128]{1,0:T(8,128)} %pad_convert_fusion.refs_0_, ...), custom_call_target="tpu_custom_call" | custom-call | tf_op jit(solution)/shard_map/pallas_call | solution.py:322
  142.2 0.9 slice_bitcast_fusion
  143.1 0.7 reshape.131.gains.refs_3_
  143.9 29.3 %shard_map.281 = (bf16[4,64,1536]{2,1,0:T(8,128)(2,1)}, f32[4,2,64,128]{3,2,1,0:T(8,128)}, bf16[832,1536]{1,0:T(8,128)(2,1)}, bf16[256,1536]{1,0:T(8,128)(2,1)},...) custom-call(s32[6]{0:T(128)} %convert_reduce_fusion.owner, ...), custom_call_target="tpu_custom_call" | custom-call | tf_op jit(solution)/shard_map/pallas_call | solution.py:477
  173.2 100.0 %shard_map.282 = (bf16[64,1536]{1,0:T(8,128)(2,1)}, f32[64,1536]{1,0:T(8,128)}, bf16[4,64,1536]{2,1,0:T(8,128)(2,1)}, f32[4,2,64,128]{3,2,1,0:T(8,128)}, bf16[15...) custom-call(bf16[4,64,1536]{2,1,0:T(8,128)(2,1)} %get-tuple-element.58.acc, ...), custom_call_target="tpu_custom_call" | custom-call | tf_op jit(solution)/shard_map/pallas_call | solution.py:829
  273.2 48.9 %shard_map.283 = (bf16[1536,1536]{1,0:T(8,128)(2,1)}, bf16[1536,1536]{1,0:T(8,128)(2,1)}, bf16[1536,1536]{1,0:T(8,128)(2,1)}, f32[768,1536]{1,0:T(8,128)}, f32[8,1536]{1,0:T(8,128)}, /*index=5*/bf16[256,1536]{1,0:T(8,128)(2,1)}) custom-call(s32[6]{0:T(128)} %convert_reduce_fusion.owner, bf16[768,1536]{1,0:T(8,128)(2,1)} %bitcast.53, ...), custom_call_target="tpu_custom_call" | custom-call | tf_op jit(solution)/shard_map/pallas_call | solution.py:595
  322.1 0.0 copy-start.6
  322.2 136.5 %shard_map.284 = (f32[64,1536]{1,0:T(8,128)}, f32[8,1536]{1,0:T(8,128)}, f32[48,1536]{1,0:T(8,128)}, f32[48,1536]{1,0:T(8,128)}, f32[48,1536]{1,0:T(8,128)}, /*i...) custom-call(bf16[1,2,2,64,1536]{4,3,2,1,0:T(8,128)(2,1)} %bitcast.66, bf16[64,1536]{1,0:T(8,128)(2,1)} %bitcast.65, ...), custom_call_target="tpu_custom_call" | custom-call | tf_op jit(solution)/shard_map/pallas_call | solution.py:1102
  458.7 0.0 copy-start.5
  458.7 0.0 copy-start.4
  458.7 0.0 copy-start.3
  458.7 0.9 constant_dynamic-slice_fusion
  459.6 0.5 slice_bitcast_fusion.1
  460.2 0.0 copy-done.6
  460.2 0.7 copy.42
  460.8 0.0 copy-start.2
  460.8 1.9 copy.43
  462.7 1.7 copy.44
  464.4 1.7 copy.45
  466.1 0.0 copy-done.5
  466.1 0.0 copy-start.1
  466.1 0.7 copy.46
  466.8 0.0 copy-done.4
  466.8 0.7 copy.47
  467.5 0.0 copy-done.3
  467.5 1.0 copy.48
  468.5 0.0 copy-done.2
  468.5 1.0 copy.49
  469.6 0.0 copy-done.1
  (2 shorter events, 0.0 us)
Async XLA Ops:
  0.6 0.7 copy-start
  322.1 138.0 %copy-start.6 = (bf16[64,1536]{1,0:T(8,128)(2,1)S(1)}, bf16[64,1536]{1,0:T(8,128)(2,1)}, u32[]{:S(2)}) copy-start(bf16[64,1536]{1,0:T(8,128)(2,1)} %get-tuple-element.64) | copy-start | bytes 589828
  458.7 7.4 %copy-start.5 = (f32[48,1536]{1,0:T(8,128)S(1)}, f32[48,1536]{1,0:T(8,128)}, u32[]{:S(2)}) copy-start(f32[48,1536]{1,0:T(8,128)} %get-tuple-element.117) | copy-start | bytes 884740
  458.7 8.1 %copy-start.4 = (f32[48,1536]{1,0:T(8,128)S(1)}, f32[48,1536]{1,0:T(8,128)}, u32[]{:S(2)}) copy-start(f32[48,1536]{1,0:T(8,128)} %get-tuple-element.118) | copy-start | bytes 884740
  458.7 8.8 %copy-start.3 = (f32[48,6144]{1,0:T(8,128)S(1)}, f32[48,6144]{1,0:T(8,128)}, u32[]{:S(2)}) copy-start(f32[48,6144]{1,0:T(8,128)} %get-tuple-element.119) | copy-start | bytes 3538948
  460.8 7.7 %copy-start.2 = (f32[192,1536]{1,0:T(8,128)S(1)}, f32[192,1536]{1,0:T(8,128)}, u32[]{:S(2)}) copy-start(f32[192,1536]{1,0:T(8,128)} %get-tuple-element.120) | copy-start | bytes 3538948
  466.1 3.5 copy-start.1
